TPU v7x, 32 devices: a whole 2x2x4 slice. The times are simulated.
32 devices in a mesh: groups: 2 (over x), region: 16 (over z, y, core).
Axes of the slice: x: 2, y: 2, z: 4, core: 2. Of those that a mesh axis runs over, the one named last changes fastest.
Arguments:
- patch_tiles: bfloat16 [512, 2, 4, 14336], P(('groups', 'region')), parts along dimension 0, may hold values from -6 to 6
- slot_lists: int32 [512, 2, 3], P(('groups', 'region')), parts along dimension 0, may hold values from -1 to 448, as said below
- blend_table: float32 [14, 14336], replicated, may hold values from 0.2 to 2
- smoothing: float32 [512, 896], P('region'), may hold values from 0.02 to 0.2
- analysis: bfloat16 [4, 1024, 896], P(None, 'groups', 'region'), parts along dimension 1, may hold values from -6 to 6
Outputs:
- crps_score: bfloat16 [4, 1024, 896], P(None, 'groups', 'region'), parts along dimension 1
- spread_skill: bfloat16 [2, 4, 1024, 896], P(None, None, 'groups', 'region'), parts along dimension 2
There are 2 independent parts, one for each index of `groups`. A program takes and returns all parts, laid end to end along the dimension named above; an argument that names none is the same for every part. Nothing has to cross between parts.
Inputs may be any that keep to these rules, and one draw needn't show every extreme that they name: `slot_lists`: row p * 16 + r lists device p's slots for region r: sample (-1 marks an empty slot), first column, blend_table row. Device p lists only tiles of sample p // 2. In a region every sample has tiles at the same columns with the same table rows; a quarter of the regions, drawn, hold 4 tiles a sample and the others 2; in each region one tile starts at column 0 and one at 448. Slot 0 of every row is live; slot 1 is live exactly in the regions with 4 tiles.
All inputs are finite; a program needn't handle non-finite values.
Results may differ from a plain program's by a relative error of at most 0.0022.
The roundings to bfloat16 on the way count: a program that leaves them out, or rounds other values in their place, can miss the bound.
Values may be sent and summed in bfloat16 or wider, within the bound.
No kernel may reach another device: no remote copies, remote signals or barrier semaphores. Data moves between devices by JAX's collectives and lax.ppermute only.
A program may use at most 192 MiB of HBM per device.

v0:
```python
import functools

import jax
import jax.numpy as jnp
from jax import lax
from jax.experimental import pallas as pl
from jax.experimental.pallas import tpu as pltpu
from jax.sharding import PartitionSpec as P

SAMPLES = 8
FIELDS = 4
PATCH = 448
CAP = 2
ROWS = 32
COLS = 896
PAIRS = ROWS // 2
FLAT = ROWS * PATCH
LANES = 128
TILES = COLS // LANES
PER_CHUNK = 2
CHUNKS = FIELDS // PER_CHUNK
MID = 0.11
VMEM = 48 * 1024 * 1024


def round_up(value, step):
    return -(-value // step) * step


class Sizes:
    def __init__(self, regions):
        self.regions = regions
        self.makers = regions // SAMPLES
        self.block = regions // self.makers
        self.heavy = min(self.block, regions // 4)
        self.part = self.block * ROWS
        self.width = COLS // regions
        self.span = round_up(self.width, 8)
        self.rows = regions * ROWS
        self.main = PER_CHUNK * self.span

    def chunk_rows(self, chunk):
        return self.main + (16 if chunk == 0 else 8)


def slot_field(region, slot, field):
    return (region * CAP + slot) * 3 + field


def pack_kernel(z, lists, tiles, packed, sems):
    part = lax.rem(lax.axis_index("region"), z.makers)
    for k in range(1, z.makers):
        first = lax.rem(part + k, z.makers) * z.block
        bulk = pltpu.make_async_copy(
            tiles.at[pl.ds(first, z.block), 0], packed.at[k - 1, pl.ds(0, z.block)], sems.at[k - 1, 0]
        )
        bulk.start()
        rank = jnp.int32(0)
        for j in range(z.block):
            live = lists[slot_field(first + j, 1, 0)] >= 0

            @pl.when(live)
            def _(j=j, rank=rank):
                pltpu.make_async_copy(
                    tiles.at[first + j, 1], packed.at[k - 1, z.block + rank], sems.at[k - 1, 1 + j]
                ).start()

            rank = jnp.minimum(rank + live.astype(jnp.int32), z.heavy - 1)
    for k in range(1, z.makers):
        first = lax.rem(part + k, z.makers) * z.block
        pltpu.make_async_copy(
            tiles.at[pl.ds(first, z.block), 0], packed.at[k - 1, pl.ds(0, z.block)], sems.at[k - 1, 0]
        ).wait()
        for j in range(z.block):

            @pl.when(lists[slot_field(first + j, 1, 0)] >= 0)
            def _(j=j):
                pltpu.make_async_copy(
                    tiles.at[first + j, 1], packed.at[k - 1, z.block], sems.at[k - 1, 1 + j]
                ).wait()


def pack_tiles(z, lists, tiles):
    return pl.pallas_call(
        functools.partial(pack_kernel, z),
        out_shape=jax.ShapeDtypeStruct((z.makers - 1, z.block + z.heavy, FIELDS, FLAT), jnp.bfloat16),
        in_specs=[pl.BlockSpec(memory_space=pltpu.SMEM), pl.BlockSpec(memory_space=pl.ANY)],
        out_specs=pl.BlockSpec(memory_space=pl.ANY),
        scratch_shapes=[pltpu.SemaphoreType.DMA((z.makers - 1, 1 + z.block))],
        name="pack_tiles",
    )(lists, tiles)


def blend_kernel(z, meta, *refs):
    slots = refs[: 2 * z.makers]
    table, smoothing = refs[2 * z.makers : 2 * z.makers + 2]
    outs = refs[2 * z.makers + 2 : 2 * z.makers + 2 + CHUNKS]
    staged, lines, turned, strength = refs[2 * z.makers + 2 + CHUNKS :]
    j = pl.program_id(0)
    quad = LANES // ROWS
    region = meta[0] * z.block + j

    def entry(maker, slot, field):
        return meta[1 + maker * z.regions * CAP * 3 + slot_field(region, slot, field)]

    heavy = entry(0, 1, 0) >= 0
    lane = lax.broadcasted_iota(jnp.int32, (PAIRS, COLS), 1)

    def stage(index):
        ref = slots[index]
        for k in range(PAIRS):
            for t in range(TILES):
                at = COLS * k + LANES * t
                staged[index, t, FIELDS * k : FIELDS * (k + 1), :] = ref[0, 0, :, at : at + LANES].astype(
                    jnp.float32
                )

    def pairs_of(index, field):
        return jnp.concatenate(
            [staged[index, t, pl.ds(field, PAIRS, stride=FIELDS), :] for t in range(TILES)], 1
        )

    def put(field, even, odd):
        at = lax.rem(j, quad) * ROWS
        for t in range(TILES):
            here = slice(LANES * t, LANES * (t + 1))
            lines[field, t, pl.ds(at, PAIRS, stride=2), :] = even[:, here]
            lines[field, t, pl.ds(at + 1, PAIRS, stride=2), :] = odd[:, here]

    for maker in range(z.makers):
        stage(2 * maker)

    def general(live_slots):
        def placed(pairs, column):
            turn = pltpu.roll(pairs, column, 1)
            other = pltpu.roll(turn, PATCH, 1)
            inside = (lane >= column) & (lane < column + PATCH)
            return jnp.where(inside, turn, 0.0), jnp.where(inside, other, 0.0)

        columns = [entry(i // 2, i % 2, 1) for i in live_slots]
        weights = [table[entry(i // 2, i % 2, 2)] for i in live_slots]
        even, odd = 0.0, 0.0
        for column, weight in zip(columns, weights):
            a, b = placed(weight, column)
            even, odd = even + a, odd + b
        even_inv, odd_inv = 1.0 / even, 1.0 / odd

        def one_field(field, carry):
            even, odd = 0.0, 0.0
            for i, column, weight in zip(live_slots, columns, weights):
                a, b = placed(pairs_of(i, field) * weight, column)
                even, odd = even + a, odd + b
            put(field, even * even_inv, odd * odd_inv)
            return carry

        lax.fori_loop(0, FIELDS, one_field, 0)

    @pl.when(heavy)
    def _():
        for maker in range(z.makers):
            stage(2 * maker + 1)
        general(list(range(2 * z.makers)))

    @pl.when(jnp.logical_not(heavy))
    def _():
        if z.makers != 2:
            general([2 * maker for maker in range(z.makers)])
            return
        left_maker = (entry(0, 0, 1) != 0).astype(jnp.int32)
        left, right = 2 * left_maker, 2 - 2 * left_maker
        left_weight = table[entry(left_maker, 0, 2)]
        right_weight = table[entry(1 - left_maker, 0, 2)]

        def merged(a, b):
            even = jnp.where(lane < PATCH, a, pltpu.roll(b, PATCH, 1))
            odd = jnp.where(lane < PATCH, pltpu.roll(a, PATCH, 1), b)
            return even, odd

        even_sum, odd_sum = merged(left_weight, right_weight)
        even_inv, odd_inv = 1.0 / even_sum, 1.0 / odd_sum

        def one_field(field, carry):
            even, odd = merged(
                pairs_of(left, field) * left_weight,
                pairs_of(right, field) * right_weight,
            )
            put(field, even * even_inv, odd * odd_inv)
            return carry

        lax.fori_loop(0, FIELDS, one_field, 0)

    @pl.when(j == 0)
    def _():
        turned_strength = jnp.transpose(smoothing[...] - MID)
        for dest in range(z.regions):
            for g in range(z.span // 8):
                top = z.width * dest + 8 * g
                rows = min(8, COLS - top)
                strength[dest, 0:rows, ROWS * g : ROWS * (g + 1)] = turned_strength[top : top + rows]

    @pl.when(lax.rem(j, quad) == quad - 1)
    def _():
        at = pl.multiple_of(lax.div(j, quad) * LANES, LANES)
        for field in range(FIELDS):
            for t in range(TILES):
                turned[field, LANES * t : LANES * (t + 1), :] = jnp.transpose(lines[field, t])
        for chunk in range(CHUNKS):
            fields = range(chunk * PER_CHUNK, (chunk + 1) * PER_CHUNK)
            for dest in range(z.regions):
                first = z.width * dest
                block = [turned[field, first : first + z.span, :] for field in fields]
                outs[chunk][dest, 0 : z.main, pl.ds(at, LANES)] = jnp.concatenate(block, 0).astype(jnp.bfloat16)
                low, high = max(first - 1, 0), min(first + z.width, COLS - 1)
                edge = [turned[field, at_row : at_row + 1, :] for field in fields for at_row in (low, high)]
                edge.append(jnp.zeros((8 - len(edge), LANES), jnp.float32))
                if chunk == 0:
                    edge.append(strength[dest, :, pl.ds(at, LANES)])
                outs[chunk][dest, z.main : z.chunk_rows(chunk), pl.ds(at, LANES)] = jnp.concatenate(
                    edge, 0
                ).astype(jnp.bfloat16)


def blend(z, meta, tiles, received, table, smoothing):
    tile_block = (1, 1, FIELDS, FLAT)

    def rank(j, meta):
        first = meta[0] * z.block
        total = jnp.int32(0)
        for before in range(z.block):
            live = meta[1 + slot_field(first + before, 1, 0)] >= 0
            total = total + jnp.where(live & (before < j), 1, 0)
        return z.block + jnp.minimum(total, z.heavy - 1)

    in_specs = [
        pl.BlockSpec(tile_block, lambda j, meta: (meta[0] * z.block + j, 0, 0, 0)),
        pl.BlockSpec(tile_block, lambda j, meta: (meta[0] * z.block + j, 1, 0, 0)),
    ]
    operands = [tiles, tiles]
    for item in received:
        in_specs += [
            pl.BlockSpec(tile_block, lambda j, meta: (0, j, 0, 0)),
            pl.BlockSpec(tile_block, lambda j, meta: (0, rank(j, meta), 0, 0)),
        ]
        operands += [item, item]
    in_specs += [
        pl.BlockSpec(table.shape, lambda j, meta: (0, 0, 0)),
        pl.BlockSpec(smoothing.shape, lambda j, meta: (0, 0)),
    ]
    shapes = [(z.regions, z.chunk_rows(chunk), z.part) for chunk in range(CHUNKS)]
    return pl.pallas_call(
        functools.partial(blend_kernel, z),
        out_shape=[jax.ShapeDtypeStruct(shape, jnp.bfloat16) for shape in shapes],
        grid_spec=pltpu.PrefetchScalarGridSpec(
            num_scalar_prefetch=1,
            grid=(z.block,),
            in_specs=in_specs,
            out_specs=[pl.BlockSpec(shape, lambda j, meta: (0, 0, 0)) for shape in shapes],
            scratch_shapes=[
                pltpu.VMEM((2 * z.makers, TILES, PAIRS * FIELDS, LANES), jnp.float32),
                pltpu.VMEM((FIELDS, TILES, LANES, LANES), jnp.float32),
                pltpu.VMEM((FIELDS, COLS + 8, LANES), jnp.float32),
                pltpu.VMEM((z.regions, 8, z.part), jnp.float32),
            ],
        ),
        compiler_params=pltpu.CompilerParams(vmem_limit_bytes=VMEM),
        name="blend",
    )(meta, *operands, table, smoothing)


SORT_STEPS = (
    ((0, 1), (2, 3), (4, 5), (6, 7)),
    ((0, 2), (1, 3), (4, 6), (5, 7)),
    ((1, 2), (5, 6)),
    ((0, 4), (1, 5), (2, 6), (3, 7)),
    ((2, 4), (3, 5)),
    ((1, 2), (3, 4), (5, 6)),
)


def score_kernel(z, chunk, block, strength_block, analysis, *refs):
    crps, spread = refs[-6:-4]
    strength, padded, members, results = refs[-4:]
    rows = z.rows
    for source in range(z.regions):
        piece = strength_block[source].astype(jnp.float32)[8:16]
        for g in range(z.span // 8):
            strength[8 * g : 8 * (g + 1), ROWS * source : ROWS * (source + 1)] = (
                piece[:, ROWS * g : ROWS * (g + 1)] + MID
            )
    lane = lax.broadcasted_iota(jnp.int32, (8, rows), 1)
    for f in range(PER_CHUNK):
        for sample in range(SAMPLES):
            for part in range(z.makers):
                source = sample * z.makers + part
                lanes = slice(part * z.part, (part + 1) * z.part)
                values = block[source, 0 : z.main, :].astype(jnp.float32)
                padded[8 : 8 + z.span, lanes] = values[f * z.span : (f + 1) * z.span]
                edge = block[source, z.main : z.main + 8, :].astype(jnp.float32)
                padded[7:8, lanes] = edge[2 * f : 2 * f + 1]
                padded[8 + z.width : 9 + z.width, lanes] = edge[2 * f + 1 : 2 * f + 2]
            for g in range(z.span // 8):
                here = padded[8 + 8 * g : 16 + 8 * g, :]
                sides = padded[7 + 8 * g : 15 + 8 * g, :] + padded[9 + 8 * g : 17 + 8 * g, :]
                above = jnp.where(lane == 0, here, pltpu.roll(here, 1, 1))
                below = jnp.where(lane == rows - 1, here, pltpu.roll(here, rows - 1, 1))
                laplace = above + below + sides - 4.0 * here
                smooth = here + strength[8 * g : 8 * (g + 1), :] * laplace
                members[sample, 8 * g : 8 * (g + 1), :] = smooth.astype(jnp.bfloat16).astype(jnp.float32)
        target_field = analysis[f].astype(jnp.float32)
        for g in range(z.span // 8):
            here = slice(8 * g, min(8 * (g + 1), z.width))
            values = [members[sample, here, :] for sample in range(SAMPLES)]
            target = target_field[here]
            error = sum(jnp.abs(value - target) for value in values) * (1.0 / SAMPLES)
            average = sum(values) * (1.0 / SAMPLES)
            variance = sum((value - average) ** 2 for value in values) * (1.0 / (SAMPLES - 1.0))
            ranked = list(values)
            for step in SORT_STEPS:
                for low, high in step:
                    a, b = ranked[low], ranked[high]
                    ranked[low], ranked[high] = jnp.minimum(a, b), jnp.maximum(a, b)
            half = SAMPLES // 2
            pairs = sum(
                (2 * k - SAMPLES + 1.0) * (ranked[k] - ranked[SAMPLES - 1 - k]) for k in range(half, SAMPLES)
            )
            results[0, here, :] = error - pairs * (1.0 / (SAMPLES * SAMPLES))
            results[1, here, :] = variance
            results[2, here, :] = (average - target) ** 2
        crps[f] = results[0, 0 : z.width, :].astype(jnp.bfloat16)
        spread[0, f] = results[1, 0 : z.width, :].astype(jnp.bfloat16)
        spread[1, f] = results[2, 0 : z.width, :].astype(jnp.bfloat16)


def score(z, chunk, block, first_block, analysis, earlier):
    width, rows = z.width, z.rows
    tail = z.main // 16
    in_specs = [
        pl.BlockSpec(block.shape, lambda i: (0, 0, 0)),
        pl.BlockSpec((z.regions, 16, z.part), lambda i: (0, tail, 0)),
        pl.BlockSpec((PER_CHUNK, width, rows), lambda i: (chunk, 0, 0)),
    ]
    in_specs += [pl.BlockSpec(memory_space=pl.ANY)] * len(earlier)
    return pl.pallas_call(
        functools.partial(score_kernel, z, chunk),
        out_shape=[
            jax.ShapeDtypeStruct((FIELDS, width, rows), jnp.bfloat16),
            jax.ShapeDtypeStruct((2, FIELDS, width, rows), jnp.bfloat16),
        ],
        grid=(1,),
        in_specs=in_specs,
        out_specs=[
            pl.BlockSpec((PER_CHUNK, width, rows), lambda i: (chunk, 0, 0)),
            pl.BlockSpec((2, PER_CHUNK, width, rows), lambda i: (0, chunk, 0, 0)),
        ],
        scratch_shapes=[
            pltpu.VMEM((z.span, rows), jnp.float32),
            pltpu.VMEM((z.span + 16, rows), jnp.float32),
            pltpu.VMEM((SAMPLES, z.span, rows), jnp.float32),
            pltpu.VMEM((3, z.span, rows), jnp.float32),
        ],
        input_output_aliases={3 + i: i for i in range(len(earlier))},
        compiler_params=pltpu.CompilerParams(vmem_limit_bytes=VMEM),
        cost_estimate=pl.CostEstimate(flops=30_000_000, bytes_accessed=3_000_000, transcendentals=0),
        name="score",
    )(block, first_block, analysis, *earlier)


def shards(patch_tiles, slot_lists, blend_table, smoothing, analysis):
    z = Sizes(lax.axis_size("region"))
    part = lax.rem(lax.axis_index("region"), z.makers)
    turns = [
        [(i, i - i % z.makers + (i + k) % z.makers) for i in range(z.regions)] for k in range(1, z.makers)
    ]
    other_lists = [lax.ppermute(slot_lists, "region", turn) for turn in turns]
    packed = pack_tiles(z, slot_lists.reshape(-1), patch_tiles)
    received = [lax.ppermute(packed[k : k + 1], "region", turn) for k, turn in enumerate(turns)]
    meta = jnp.concatenate([part.reshape(1)] + [item.reshape(-1) for item in [slot_lists, *other_lists]])
    table = blend_table.reshape(blend_table.shape[0], PAIRS, COLS)
    blocks = blend(z, meta, patch_tiles, received, table, smoothing)
    moved = [lax.all_to_all(item, "region", split_axis=0, concat_axis=0, tiled=True) for item in blocks]
    analysis = jnp.swapaxes(analysis, 1, 2)
    outs = ()
    for chunk in range(CHUNKS):
        outs = score(z, chunk, moved[chunk], moved[0], analysis, outs)
    return tuple(jnp.swapaxes(item, -1, -2) for item in outs)


def solution(mesh):
    return jax.shard_map(
        shards,
        mesh=mesh,
        in_specs=(
            P(("groups", "region"), None, None, None),
            P(("groups", "region"), None, None),
            P(),
            P("region", None),
            P(None, "groups", "region"),
        ),
        out_specs=(P(None, "groups", "region"), P(None, None, "groups", "region")),
        check_vma=False,
    )
```

profile of v0, /device:TPU:1, one launch (start us, length us, event | category | flops | bytes accessed | tf_op | source)
XLA Modules:
  0.0 118.9 jit_solution(6857935179439479258)
XLA Ops:
  0.6 0.8 copy.11
  1.4 0.6 reshape.18.lists
  2.0 0.0 copy-start.4
  2.0 40.2 %pack_tiles.1 = bf16[1,12,4,14336]{3,2,1,0:T(4,128)(2,1)} custom-call(s32[96]{0:T(128)} %reshape.18.lists, bf16[16,2,4,14336]{3,2,1,0:T(4,128)(2,1)} %refs_1_.1), custom_call_target="tpu_custom_call" | custom-call | tf_op jit(solution)/shard_map/pack_tiles/pallas_call | solution.py:84
  42.2 0.1 collective-permute-start.1
  42.3 0.0 copy-done.4
  42.3 0.5 collective-permute-start
  42.8 0.0 copy-done.2
  42.8 0.2 copy.13
  43.0 0.1 slice.refs_4_
  43.1 2.0 %collective-permute-done = s32[16,2,3]{0,1,2:T(2,128)S(1)} collective-permute-done((s32[16,2,3]{0,1,2:T(2,128)S(1)}, s32[16,2,3]{0,1,2:T(2,128)S(1)}, u32[]{:S(2)}, u32[]{:S(2)}) %collective-permute-start) | collective-permute-done | bytes 416 | tf_op jit(solution)/shard_map/ppermute | solution.py:374
  45.1 0.1 copy.12
  45.2 0.1 reshape.19
  45.3 0.0 copy-done.3
  45.3 0.1 pad_add_fusion.meta
  45.4 0.3 collective-permute-done.1.refs_2_.refs_3_
  45.7 0.0 copy-done.1
  45.7 10.0 %blend.1 = (bf16[16,128,256]{2,1,0:T(8,128)(2,1)S(1)}, bf16[16,120,256]{2,1,0:T(8,128)(2,1)}) custom-call(s32[193]{0:T(256)S(1)} %pad_add_fusion.meta, bf16[16,2,4,14336]{3,2,1,0:T(4,128)(2,1)} %refs_1_.1, bf16[16,2,4,14336]{3,2,1,0:T(4,128)(2,1)} %refs_1_.1, bf16[1,12,4,14336]{3,2,1,0:T(4,128)(2,1)S(1)} %collective-permute-done.1.refs_2_.refs_3_, ...), custom_call_target="tpu_custom_call" | custom-call | tf_op jit(solution)/shard_map/blend/pallas_call | solution.py:250
  55.7 33.2 %all_to_all.10.block.strength_block = bf16[16,128,256]{2,1,0:T(8,128)(2,1)S(1)} all-to-all(bf16[16,128,256]{2,1,0:T(8,128)(2,1)S(1)} %get-tuple-element.9), channel_id=1, replica_groups=mesh['groups'=2,'region'=16] {'region'}, dimensions={0} | all-to-all | bytes 2097152 | tf_op jit(solution)/shard_map/all_to_all | solution.py:380
  88.9 4.8 %all-to-all-start = ((bf16[16,120,256]{2,1,0:T(8,128)(2,1)}), bf16[16,120,256]{2,1,0:T(8,128)(2,1)S(1)}, u32[]{:S(2)}, u32[]{:S(2)}) async-start(bf16[16,120,256]{2,1,0:T(8,128)(2,1)} %get-tuple-element.8), calls=%async_computation | async-start | bytes 1966080 | tf_op jit(solution)/shard_map/all_to_all | solution.py:380
  93.7 0.0 copy-done
  93.7 3.3 %score.2 = (bf16[4,56,512]{2,1,0:T(8,128)(2,1)}, bf16[2,4,56,512]{3,2,1,0:T(8,128)(2,1)}) custom-call(bf16[16,128,256]{2,1,0:T(8,128)(2,1)S(1)} %all_to_all.10.block.strength_block, bf16[16,128,256]{2,1,0:T(8,128)(2,1)S(1)} %all_to_all.10.block.strength_block, bf16[4,56,512]{2,1,0:T(8,128)(2,1)S(1)} %bitcast.7), custom_call_target="tpu_custom_call" | custom-call | flops 30000000 | bytes 3000000 | tf_op jit(solution)/shard_map/score/pallas_call | solution.py:343
  97.0 18.7 %all-to-all-done.block = bf16[16,120,256]{2,1,0:T(8,128)(2,1)S(1)} async-done(((bf16[16,120,256]{2,1,0:T(8,128)(2,1)}), bf16[16,120,256]{2,1,0:T(8,128)(2,1)S(1)}, u32[]{:S(2)}, u32[]{:S(2)}) %all-to-all-start) | async-done | bytes 983072 | tf_op jit(solution)/shard_map/all_to_all | solution.py:380
  115.7 3.3 %score.3 = (bf16[4,56,512]{2,1,0:T(8,128)(2,1)}, bf16[2,4,56,512]{3,2,1,0:T(8,128)(2,1)}) custom-call(bf16[16,120,256]{2,1,0:T(8,128)(2,1)S(1)} %all-to-all-done.block, bf16[16,128,256]{2,1,0:T(8,128)(2,1)S(1)} %all_to_all.10.block.strength_block, bf16[4,56,512]{2,1,0:T(8,128)(2,1)S(1)} %bitcast.8, ...), custom_call_target="tpu_custom_call", output_to_operand_aliasing={{0}: (3, {}), {1}: (4, {})} | custom-call | flops 30000000 | bytes 3000000 | tf_op jit(solution)/shard_map/score/pallas_call | solution.py:343
  (4 shorter events, 0.0 us)
Async XLA Ops:
  2.0 40.3 %copy-start.4 = (s32[16,2,3]{0,1,2:T(2,128)S(1)}, s32[16,2,3]{0,1,2:T(2,128)}, u32[]{:S(2)}) copy-start(s32[16,2,3]{0,1,2:T(2,128)} %param.6) | copy-start | bytes 1156
  2.0 40.8 %copy-start.2 = (f32[14,14336]{1,0:T(8,128)S(1)}, f32[14,14336]{1,0:T(8,128)}, u32[]{:S(2)}) copy-start(f32[14,14336]{1,0:T(8,128)} %param.7) | copy-start | bytes 2408452
  42.2 3.4 %collective-permute-start.1 = (bf16[1,12,4,14336]{3,2,1,0:T(4,128)(2,1)}, bf16[1,12,4,14336]{3,2,1,0:T(4,128)(2,1)S(1)}, u32[]{:S(2)}, u32[]{:S(2)}) collective-permute-start(bf16[1,12,4,14336]{3,2,1,0:T(4,128)(2,1)} %pack_tiles.1), channel_id=1, source_target_pairs={{0,1},{1,0},{2,3},{3,2},{4,5},{5,4},{6,7},{7,6},{8,9},{9,8},{10,11... | collective-permute-start | bytes 4128776 | tf_op jit(solution)/shard_map/ppermute | solution.py:376
  42.3 2.7 %collective-permute-start = (s32[16,2,3]{0,1,2:T(2,128)S(1)}, s32[16,2,3]{0,1,2:T(2,128)S(1)}, u32[]{:S(2)}, u32[]{:S(2)}) collective-permute-start(s32[16,2,3]{0,1,2:T(2,128)S(1)} %copy-done.4), channel_id=1, source_target_pairs={{0,1},{1,0},{2,3},{3,2},{4,5},{5,4},{6,7},{7,6},{8,9},{9,8},{10,11... | collective-permute-start | bytes 1160 | tf_op jit(solution)/shard_map/ppermute | solution.py:374
  42.8 2.5 %copy-start.3 = (s32[96]{0:T(128)S(1)}, s32[96]{0:T(128)}, u32[]{:S(2)}) copy-start(s32[96]{0:T(128)} %reshape.18.lists) | copy-start | bytes 1156
  42.8 2.8 %copy-start.1 = (f32[32,896]{1,0:T(8,128)S(1)}, f32[32,896]{1,0:T(8,128)}, u32[]{:S(2)}) copy-start(f32[32,896]{1,0:T(8,128)} %refs_5_.1) | copy-start | bytes 344068
  88.9 4.8 %copy-start = (bf16[4,512,56]{1,2,0:T(8,128)(2,1)S(1)}, bf16[4,512,56]{1,2,0:T(8,128)(2,1)}, u32[]{:S(2)}) copy-start(bf16[4,512,56]{1,2,0:T(8,128)(2,1)} %param.9) | copy-start | bytes 688132
  88.9 26.7 %all-to-all-start = ((bf16[16,120,256]{2,1,0:T(8,128)(2,1)}), bf16[16,120,256]{2,1,0:T(8,128)(2,1)S(1)}, u32[]{:S(2)}, u32[]{:S(2)}) async-start(bf16[16,120,256]{2,1,0:T(8,128)(2,1)} %get-tuple-element.8), calls=%async_computation | async-start | bytes 1966080 | tf_op jit(solution)/shard_map/all_to_all | solution.py:380
where the time goes:
time: 120 us; the launch traced here: 119 us
  Pallas kernels  56.8 us (47%)
  blocking collectives  33.2 us (28%)
  waiting for transfers between devices  21 us (18%)
  starting transfers between devices  5.33 us (4%)
  local copies, waits for them, and re-layouts  1.86 us (2%)
    pallas_call x1, Pallas kernels, pack_tiles(): pl.pallas_call(functools.partial(pack_kernel, z), out_shape=jax.ShapeDtyp...  40.2 us
    all_to_all x1, blocking collectives, shards(): lax.all_to_all(item, 'region', split_axis=0, concat_axis=0, tiled=True)  33.2 us
    all_to_all x1, waiting for transfers between devices, shards(): lax.all_to_all(item, 'region', split_axis=0, concat_axis=0, tiled=True)  18.7 us
    pallas_call x1, Pallas kernels, blend(): pl.pallas_call(functools.partial(blend_kernel, z), out_shape=[jax.ShapeDt...  10 us
    pallas_call x2, Pallas kernels, score(): pl.pallas_call(functools.partial(score_kernel, z, chunk), out_shape=[jax....  6.55 us
    all_to_all x1, starting transfers between devices, shards(): lax.all_to_all(item, 'region', split_axis=0, concat_axis=0, tiled=True)  4.77 us
  transfers between devices with their start and end apart: 3, of which 3 were waited for; matrix products, arithmetic and copies ran while one was open for 0% of the time, Pallas kernels for 3%

commit v1 on v0

--- a/solution.py
+++ b/solution.py
@@ -43,10 +43,6 @@
         return self.main + (16 if chunk == 0 else 8)
 
 
-def slot_field(region, slot, field):
-    return (region * CAP + slot) * 3 + field
-
-
 def pack_kernel(z, lists, tiles, packed, sems):
     part = lax.rem(lax.axis_index("region"), z.makers)
     for k in range(1, z.makers):
@@ -57,7 +53,7 @@
         bulk.start()
         rank = jnp.int32(0)
         for j in range(z.block):
-            live = lists[slot_field(first + j, 1, 0)] >= 0
+            live = lists[0, 1, first + j] >= 0
 
             @pl.when(live)
             def _(j=j, rank=rank):
@@ -73,7 +69,7 @@
         ).wait()
         for j in range(z.block):
 
-            @pl.when(lists[slot_field(first + j, 1, 0)] >= 0)
+            @pl.when(lists[0, 1, first + j] >= 0)
             def _(j=j):
                 pltpu.make_async_copy(
                     tiles.at[first + j, 1], packed.at[k - 1, z.block], sems.at[k - 1, 1 + j]
@@ -85,23 +81,24 @@
         functools.partial(pack_kernel, z),
         out_shape=jax.ShapeDtypeStruct((z.makers - 1, z.block + z.heavy, FIELDS, FLAT), jnp.bfloat16),
         in_specs=[pl.BlockSpec(memory_space=pltpu.SMEM), pl.BlockSpec(memory_space=pl.ANY)],
-        out_specs=pl.BlockSpec(memory_space=pl.ANY),
+        out_specs=pl.BlockSpec(memory_space=pltpu.VMEM),
         scratch_shapes=[pltpu.SemaphoreType.DMA((z.makers - 1, 1 + z.block))],
+        compiler_params=pltpu.CompilerParams(vmem_limit_bytes=VMEM),
         name="pack_tiles",
     )(lists, tiles)
 
 
-def blend_kernel(z, meta, *refs):
+def blend_kernel(z, chunk, part, *refs):
+    lists, refs = refs[: z.makers], refs[z.makers :]
     slots = refs[: 2 * z.makers]
-    table, smoothing = refs[2 * z.makers : 2 * z.makers + 2]
-    outs = refs[2 * z.makers + 2 : 2 * z.makers + 2 + CHUNKS]
-    staged, lines, turned, strength = refs[2 * z.makers + 2 + CHUNKS :]
+    table, smoothing, out, staged, lines, turned, strength = refs[2 * z.makers :]
+    fields = range(chunk * PER_CHUNK, (chunk + 1) * PER_CHUNK)
     j = pl.program_id(0)
     quad = LANES // ROWS
-    region = meta[0] * z.block + j
+    region = part[0] * z.block + j
 
     def entry(maker, slot, field):
-        return meta[1 + maker * z.regions * CAP * 3 + slot_field(region, slot, field)]
+        return lists[maker][field, slot, region]
 
     heavy = entry(0, 1, 0) >= 0
     lane = lax.broadcasted_iota(jnp.int32, (PAIRS, COLS), 1)
@@ -124,8 +121,8 @@
         at = lax.rem(j, quad) * ROWS
         for t in range(TILES):
             here = slice(LANES * t, LANES * (t + 1))
-            lines[field, t, pl.ds(at, PAIRS, stride=2), :] = even[:, here]
-            lines[field, t, pl.ds(at + 1, PAIRS, stride=2), :] = odd[:, here]
+            lines[field - fields.start, t, pl.ds(at, PAIRS, stride=2), :] = even[:, here]
+            lines[field - fields.start, t, pl.ds(at + 1, PAIRS, stride=2), :] = odd[:, here]
 
     for maker in range(z.makers):
         stage(2 * maker)
@@ -153,7 +150,7 @@
             put(field, even * even_inv, odd * odd_inv)
             return carry
 
-        lax.fori_loop(0, FIELDS, one_field, 0)
+        lax.fori_loop(fields.start, fields.stop, one_field, 0)
 
     @pl.when(heavy)
     def _():
@@ -168,8 +165,9 @@
             return
         left_maker = (entry(0, 0, 1) != 0).astype(jnp.int32)
         left, right = 2 * left_maker, 2 - 2 * left_maker
-        left_weight = table[entry(left_maker, 0, 2)]
-        right_weight = table[entry(1 - left_maker, 0, 2)]
+        own, other = entry(0, 0, 2), entry(1, 0, 2)
+        left_weight = table[jnp.where(left_maker == 0, own, other)]
+        right_weight = table[jnp.where(left_maker == 0, other, own)]
 
         def merged(a, b):
             even = jnp.where(lane < PATCH, a, pltpu.roll(b, PATCH, 1))
@@ -187,9 +185,9 @@
             put(field, even * even_inv, odd * odd_inv)
             return carry
 
-        lax.fori_loop(0, FIELDS, one_field, 0)
-
-    @pl.when(j == 0)
+        lax.fori_loop(fields.start, fields.stop, one_field, 0)
+
+    @pl.when((j == 0) & (chunk == 0))
     def _():
         turned_strength = jnp.transpose(smoothing[...] - MID)
         for dest in range(z.regions):
@@ -201,70 +199,67 @@
     @pl.when(lax.rem(j, quad) == quad - 1)
     def _():
         at = pl.multiple_of(lax.div(j, quad) * LANES, LANES)
-        for field in range(FIELDS):
+        for f in range(PER_CHUNK):
             for t in range(TILES):
-                turned[field, LANES * t : LANES * (t + 1), :] = jnp.transpose(lines[field, t])
-        for chunk in range(CHUNKS):
-            fields = range(chunk * PER_CHUNK, (chunk + 1) * PER_CHUNK)
-            for dest in range(z.regions):
-                first = z.width * dest
-                block = [turned[field, first : first + z.span, :] for field in fields]
-                outs[chunk][dest, 0 : z.main, pl.ds(at, LANES)] = jnp.concatenate(block, 0).astype(jnp.bfloat16)
-                low, high = max(first - 1, 0), min(first + z.width, COLS - 1)
-                edge = [turned[field, at_row : at_row + 1, :] for field in fields for at_row in (low, high)]
-                edge.append(jnp.zeros((8 - len(edge), LANES), jnp.float32))
-                if chunk == 0:
-                    edge.append(strength[dest, :, pl.ds(at, LANES)])
-                outs[chunk][dest, z.main : z.chunk_rows(chunk), pl.ds(at, LANES)] = jnp.concatenate(
-                    edge, 0
-                ).astype(jnp.bfloat16)
-
-
-def blend(z, meta, tiles, received, table, smoothing):
+                turned[f, LANES * t : LANES * (t + 1), :] = jnp.transpose(lines[f, t])
+        for dest in range(z.regions):
+            first = z.width * dest
+            block = [turned[f, first : first + z.span, :] for f in range(PER_CHUNK)]
+            out[dest, 0 : z.main, pl.ds(at, LANES)] = jnp.concatenate(block, 0).astype(jnp.bfloat16)
+            ends = (max(first - 1, 0), min(first + z.width, COLS - 1))
+            edge = [turned[f, end : end + 1, :] for f in range(PER_CHUNK) for end in ends]
+            edge.append(jnp.zeros((8 - len(edge), LANES), jnp.float32))
+            if chunk == 0:
+                edge.append(strength[dest, :, pl.ds(at, LANES)])
+            edge = jnp.concatenate(edge, 0).astype(jnp.bfloat16)
+            out[dest, z.main : z.chunk_rows(chunk), pl.ds(at, LANES)] = edge
+
+
+def blend(z, chunk, part, lists, tiles, received, table, smoothing):
     tile_block = (1, 1, FIELDS, FLAT)
 
-    def rank(j, meta):
-        first = meta[0] * z.block
+    def rank(j, part, own, *others):
         total = jnp.int32(0)
         for before in range(z.block):
-            live = meta[1 + slot_field(first + before, 1, 0)] >= 0
+            live = own[0, 1, part[0] * z.block + before] >= 0
             total = total + jnp.where(live & (before < j), 1, 0)
         return z.block + jnp.minimum(total, z.heavy - 1)
 
     in_specs = [
-        pl.BlockSpec(tile_block, lambda j, meta: (meta[0] * z.block + j, 0, 0, 0)),
-        pl.BlockSpec(tile_block, lambda j, meta: (meta[0] * z.block + j, 1, 0, 0)),
+        pl.BlockSpec(tile_block, lambda j, part, *lists: (part[0] * z.block + j, 0, 0, 0)),
+        pl.BlockSpec(tile_block, lambda j, part, *lists: (part[0] * z.block + j, 1, 0, 0)),
     ]
     operands = [tiles, tiles]
     for item in received:
         in_specs += [
-            pl.BlockSpec(tile_block, lambda j, meta: (0, j, 0, 0)),
-            pl.BlockSpec(tile_block, lambda j, meta: (0, rank(j, meta), 0, 0)),
+            pl.BlockSpec(tile_block, lambda j, *scalars: (0, j, 0, 0)),
+            pl.BlockSpec(tile_block, lambda j, *scalars: (0, rank(j, *scalars), 0, 0)),
         ]
         operands += [item, item]
     in_specs += [
-        pl.BlockSpec(table.shape, lambda j, meta: (0, 0, 0)),
-        pl.BlockSpec(smoothing.shape, lambda j, meta: (0, 0)),
-    ]
-    shapes = [(z.regions, z.chunk_rows(chunk), z.part) for chunk in range(CHUNKS)]
+        pl.BlockSpec(table.shape, lambda j, *scalars: (0, 0, 0)),
+        pl.BlockSpec(smoothing.shape, lambda j, *scalars: (0, 0)),
+    ]
+    shape = (z.regions, z.chunk_rows(chunk), z.part)
     return pl.pallas_call(
-        functools.partial(blend_kernel, z),
-        out_shape=[jax.ShapeDtypeStruct(shape, jnp.bfloat16) for shape in shapes],
+        functools.partial(blend_kernel, z, chunk),
+        out_shape=jax.ShapeDtypeStruct(shape, jnp.bfloat16),
         grid_spec=pltpu.PrefetchScalarGridSpec(
-            num_scalar_prefetch=1,
+            num_scalar_prefetch=1 + z.makers,
             grid=(z.block,),
             in_specs=in_specs,
-            out_specs=[pl.BlockSpec(shape, lambda j, meta: (0, 0, 0)) for shape in shapes],
+            out_specs=pl.BlockSpec(shape, lambda j, *scalars: (0, 0, 0)),
             scratch_shapes=[
                 pltpu.VMEM((2 * z.makers, TILES, PAIRS * FIELDS, LANES), jnp.float32),
-                pltpu.VMEM((FIELDS, TILES, LANES, LANES), jnp.float32),
-                pltpu.VMEM((FIELDS, COLS + 8, LANES), jnp.float32),
+                pltpu.VMEM((PER_CHUNK, TILES, LANES, LANES), jnp.float32),
+                pltpu.VMEM((PER_CHUNK, COLS + 8, LANES), jnp.float32),
                 pltpu.VMEM((z.regions, 8, z.part), jnp.float32),
             ],
         ),
         compiler_params=pltpu.CompilerParams(vmem_limit_bytes=VMEM),
+        cost_estimate=pl.CostEstimate(flops=50_000_000, bytes_accessed=4_000_000, transcendentals=0),
         name="blend",
-    )(meta, *operands, table, smoothing)
+    )(part, *lists, *operands, table, smoothing)
 
 
 SORT_STEPS = (
@@ -371,12 +366,15 @@
     turns = [
         [(i, i - i % z.makers + (i + k) % z.makers) for i in range(z.regions)] for k in range(1, z.makers)
     ]
-    other_lists = [lax.ppermute(slot_lists, "region", turn) for turn in turns]
-    packed = pack_tiles(z, slot_lists.reshape(-1), patch_tiles)
+    lists = jnp.transpose(slot_lists, (2, 1, 0))
+    lists = [lists] + [lax.ppermute(lists, "region", turn) for turn in turns]
+    packed = pack_tiles(z, lists[0], patch_tiles)
     received = [lax.ppermute(packed[k : k + 1], "region", turn) for k, turn in enumerate(turns)]
-    meta = jnp.concatenate([part.reshape(1)] + [item.reshape(-1) for item in [slot_lists, *other_lists]])
     table = blend_table.reshape(blend_table.shape[0], PAIRS, COLS)
-    blocks = blend(z, meta, patch_tiles, received, table, smoothing)
+    blocks = [
+        blend(z, chunk, part.reshape(1), lists, patch_tiles, received, table, smoothing)
+        for chunk in range(CHUNKS)
+    ]
     moved = [lax.all_to_all(item, "region", split_axis=0, concat_axis=0, tiled=True) for item in blocks]
     analysis = jnp.swapaxes(analysis, 1, 2)
     outs = ()

time: 120 us -> 81.7 us (0.68)
  blocking collectives: 33.2 us -> 0 us
  Pallas kernels: 56.8 us -> 25.2 us
  waiting for transfers between devices: 21 us -> 35.4 us
  starting transfers between devices: 5.33 us -> 14.6 us
  local copies, waits for them, and re-layouts: 1.86 us -> 4.23 us
    pallas_call x1, Pallas kernels: 40.2 us -> 2.37 us  [pack_tiles(): pl.pallas_call(functools.partial(pack_kernel, z), out_shape=jax.ShapeDtyp...]
    all_to_all x1 -> x0, blocking collectives: 33.2 us -> none  [shards(): lax.all_to_all(item, 'region', split_axis=0, concat_axis=0, tiled=True)]
    all_to_all x1 -> x2, waiting for transfers between devices: 18.7 us -> 32.8 us  [shards(): lax.all_to_all(item, 'region', split_axis=0, concat_axis=0, tiled=True)]
    all_to_all x1 -> x2, starting transfers between devices: 4.77 us -> 14.1 us  [shards(): lax.all_to_all(item, 'region', split_axis=0, concat_axis=0, tiled=True)]
    pallas_call x1 -> x2, Pallas kernels: 10 us -> 16.3 us  [blend(): pl.pallas_call(functools.partial(blend_kernel, z, chunk), out_shape=jax.S...]
    unnamed x12 -> x13, local copies, waits for them, and re-layouts: 0.97 us -> 4.17 us
  transfers between devices with their start and end apart: 3 -> 4, of which waited for: 3 -> 3; matrix products, arithmetic and copies ran while one was open for 0% -> 0% of each run, Pallas kernels for 3% -> 14%
where the time goes in v1:
time: 81.7 us; the launch traced here: 80.2 us
  waiting for transfers between devices  35.4 us (43%)
  Pallas kernels  25.2 us (31%)
  starting transfers between devices  14.6 us (18%)
  local copies, waits for them, and re-layouts  4.23 us (5%)
    all_to_all x2, waiting for transfers between devices, shards(): lax.all_to_all(item, 'region', split_axis=0, concat_axis=0, tiled=True)  32.8 us
    pallas_call x2, Pallas kernels, blend(): pl.pallas_call(functools.partial(blend_kernel, z, chunk), out_shape=jax.S...  16.3 us
    all_to_all x2, starting transfers between devices, shards(): lax.all_to_all(item, 'region', split_axis=0, concat_axis=0, tiled=True)  14.1 us
    pallas_call x2, Pallas kernels, score(): pl.pallas_call(functools.partial(score_kernel, z, chunk), out_shape=[jax....  6.55 us
    unnamed x13, local copies, waits for them, and re-layouts  4.17 us
    ppermute x1, waiting for transfers between devices, shards(): lists = [lists] + [lax.ppermute(lists, 'region', turn) for turn in turns]  2.58 us
    pallas_call x1, Pallas kernels, pack_tiles(): pl.pallas_call(functools.partial(pack_kernel, z), out_shape=jax.ShapeDtyp...  2.37 us
  transfers between devices with their start and end apart: 4, of which 3 were waited for; matrix products, arithmetic and copies ran while one was open for 0% of the time, Pallas kernels for 14%

profile of v1, /device:TPU:1, one launch (start us, length us, event | category | flops | bytes accessed | tf_op | source)
XLA Modules:
  0.0 80.2 jit_solution(7551610338558995063)
XLA Ops:
  0.6 0.0 copy-start
  0.6 2.0 %copy-done = bf16[16,2,4,14336]{3,2,1,0:T(4,128)(2,1)S(1)} copy-done((bf16[16,2,4,14336]{3,2,1,0:T(4,128)(2,1)S(1)}, bf16[16,2,4,14336]{3,2,1,0:T(4,128)(2,1)}, u32[]{:S(2)}) %copy-start) | copy-done | bytes 3670040
  2.7 2.4 %pack_tiles.1 = bf16[1,12,4,14336]{3,2,1,0:T(4,128)(2,1)} custom-call(s32[3,2,16]{2,1,0:T(2,128)} %bitcast.1.lists.refs_0_, bf16[16,2,4,14336]{3,2,1,0:T(4,128)(2,1)S(1)} %copy-done), custom_call_target="tpu_custom_call" | custom-call | tf_op jit(solution)/shard_map/pack_tiles/pallas_call | solution.py:80
  5.1 0.4 collective-permute-start.1
  5.5 0.2 collective-permute-start
  5.6 0.0 copy-done.5
  5.6 0.2 copy.9
  5.8 0.1 slice.refs_6_
  5.9 2.6 %collective-permute-done.refs_1_ = s32[3,2,16]{2,1,0:T(2,128)S(1)} collective-permute-done((s32[3,2,16]{2,1,0:T(2,128)}, s32[3,2,16]{2,1,0:T(2,128)S(1)}, u32[]{:S(2)}, u32[]{:S(2)}) %collective-permute-start) | collective-permute-done | bytes 416 | tf_op jit(solution)/shard_map/ppermute | solution.py:370
  8.5 0.0 collective-permute-done.1.refs_4_.refs_5_
  8.5 0.0 copy-done.4
  8.5 8.3 %blend.3 = bf16[16,128,256]{2,1,0:T(8,128)(2,1)S(1)} custom-call(s32[1]{0:T(128)} %bitcast.part, s32[3,2,16]{2,1,0:T(2,128)} %bitcast.1.lists.refs_0_, s32[3,2,16]{2,1,0:T(2,128)S(1)} %collective-permute-done.refs_1_, bf16[16,2,4,14336]{3,2,1,0:T(4,128)(2,1)} %refs_3_.3, bf16[16,2,4,14336]{3,2,1,0:T(4,128)(2,1)} %refs_3_.3, ...), custom_call_target="tpu_custom_call" | custom-call | flops 50000000 | bytes 4000000 | tf_op jit(solution)/shard_map/blend/pallas_call | solution.py:244
  16.8 0.0 copy-start.1
  16.8 1.0 %copy-done.1 = bf16[16,128,256]{2,1,0:T(8,128)(2,1)} copy-done((bf16[16,128,256]{2,1,0:T(8,128)(2,1)}, bf16[16,128,256]{2,1,0:T(8,128)(2,1)S(1)}, u32[]{:S(2)}) %copy-start.1) | copy-done | bytes 1048600
  17.7 7.4 %all-to-all-start.1 = ((bf16[16,128,256]{2,1,0:T(8,128)(2,1)}), bf16[16,128,256]{2,1,0:T(8,128)(2,1)S(1)}, u32[]{:S(2)}, u32[]{:S(2)}) async-start(bf16[16,128,256]{2,1,0:T(8,128)(2,1)} %copy-done.1), calls=%async_computation.1 | async-start | bytes 2097152 | tf_op jit(solution)/shard_map/all_to_all | solution.py:378
  25.1 8.0 %blend.2 = bf16[16,120,256]{2,1,0:T(8,128)(2,1)S(1)} custom-call(s32[1]{0:T(128)} %bitcast.part, s32[3,2,16]{2,1,0:T(2,128)} %bitcast.1.lists.refs_0_, s32[3,2,16]{2,1,0:T(2,128)S(1)} %collective-permute-done.refs_1_, bf16[16,2,4,14336]{3,2,1,0:T(4,128)(2,1)} %refs_3_.3, bf16[16,2,4,14336]{3,2,1,0:T(4,128)(2,1)} %refs_3_.3, ...), custom_call_target="tpu_custom_call" | custom-call | flops 50000000 | bytes 4000000 | tf_op jit(solution)/shard_map/blend/pallas_call | solution.py:244
  33.1 0.0 copy-start.2
  33.1 1.0 %copy-done.2 = bf16[16,120,256]{2,1,0:T(8,128)(2,1)} copy-done((bf16[16,120,256]{2,1,0:T(8,128)(2,1)}, bf16[16,120,256]{2,1,0:T(8,128)(2,1)S(1)}, u32[]{:S(2)}) %copy-start.2) | copy-done | bytes 983064
  34.1 14.1 %all-to-all-done.1.block.strength_block = bf16[16,128,256]{2,1,0:T(8,128)(2,1)S(1)} async-done(((bf16[16,128,256]{2,1,0:T(8,128)(2,1)}), bf16[16,128,256]{2,1,0:T(8,128)(2,1)S(1)}, u32[]{:S(2)}, u32[]{:S(2)}) %all-to-all-start.1) | async-done | bytes 1048608 | tf_op jit(solution)/shard_map/all_to_all | solution.py:378
  48.3 6.7 %all-to-all-start = ((bf16[16,120,256]{2,1,0:T(8,128)(2,1)}), bf16[16,120,256]{2,1,0:T(8,128)(2,1)S(1)}, u32[]{:S(2)}, u32[]{:S(2)}) async-start(bf16[16,120,256]{2,1,0:T(8,128)(2,1)} %copy-done.2), calls=%async_computation | async-start | bytes 1966080 | tf_op jit(solution)/shard_map/all_to_all | solution.py:378
  54.9 0.0 copy-done.3
  55.0 3.3 %score.2 = (bf16[4,56,512]{2,1,0:T(8,128)(2,1)}, bf16[2,4,56,512]{3,2,1,0:T(8,128)(2,1)}) custom-call(bf16[16,128,256]{2,1,0:T(8,128)(2,1)S(1)} %all-to-all-done.1.block.strength_block, bf16[16,128,256]{2,1,0:T(8,128)(2,1)S(1)} %all-to-all-done.1.block.strength_block, bf16[4,56,512]{2,1,0:T(8,128)(2,1)S(1)} %bitcast.8), custom_call_target="tpu_custom_call" | custom-call | flops 30000000 | bytes 3000000 | tf_op jit(solution)/shard_map/score/pallas_call | solution.py:338
  58.2 18.7 %all-to-all-done.block = bf16[16,120,256]{2,1,0:T(8,128)(2,1)S(1)} async-done(((bf16[16,120,256]{2,1,0:T(8,128)(2,1)}), bf16[16,120,256]{2,1,0:T(8,128)(2,1)S(1)}, u32[]{:S(2)}, u32[]{:S(2)}) %all-to-all-start) | async-done | bytes 983072 | tf_op jit(solution)/shard_map/all_to_all | solution.py:378
  76.9 3.3 %score.3 = (bf16[4,56,512]{2,1,0:T(8,128)(2,1)}, bf16[2,4,56,512]{3,2,1,0:T(8,128)(2,1)}) custom-call(bf16[16,120,256]{2,1,0:T(8,128)(2,1)S(1)} %all-to-all-done.block, bf16[16,128,256]{2,1,0:T(8,128)(2,1)S(1)} %all-to-all-done.1.block.strength_block, bf16[4,56,512]{2,1,0:T(8,128)(2,1)S(1)} %bitcast.9, ...), custom_call_target="tpu_custom_call", output_to_operand_aliasing={{0}: (3, {}), {1}: (4, {})} | custom-call | flops 30000000 | bytes 3000000 | tf_op jit(solution)/shard_map/score/pallas_call | solution.py:338
  (3 shorter events, 0.0 us)
Async XLA Ops:
  0.6 2.0 %copy-start = (bf16[16,2,4,14336]{3,2,1,0:T(4,128)(2,1)S(1)}, bf16[16,2,4,14336]{3,2,1,0:T(4,128)(2,1)}, u32[]{:S(2)}) copy-start(bf16[16,2,4,14336]{3,2,1,0:T(4,128)(2,1)} %refs_3_.3) | copy-start | bytes 11010052
  2.7 3.0 %copy-start.5 = (f32[14,14336]{1,0:T(8,128)S(1)}, f32[14,14336]{1,0:T(8,128)}, u32[]{:S(2)}) copy-start(f32[14,14336]{1,0:T(8,128)} %param.7) | copy-start | bytes 2408452
  5.1 3.4 %collective-permute-start.1 = (bf16[1,12,4,14336]{3,2,1,0:T(4,128)(2,1)}, bf16[1,12,4,14336]{3,2,1,0:T(4,128)(2,1)S(1)}, u32[]{:S(2)}, u32[]{:S(2)}) collective-permute-start(bf16[1,12,4,14336]{3,2,1,0:T(4,128)(2,1)} %pack_tiles.1), channel_id=1, source_target_pairs={{0,1},{1,0},{2,3},{3,2},{4,5},{5,4},{6,7},{7,6},{8,9},{9,8},{10,11... | collective-permute-start | bytes 4128776 | tf_op jit(solution)/shard_map/ppermute | solution.py:372
  5.5 3.0 %collective-permute-start = (s32[3,2,16]{2,1,0:T(2,128)}, s32[3,2,16]{2,1,0:T(2,128)S(1)}, u32[]{:S(2)}, u32[]{:S(2)}) collective-permute-start(s32[3,2,16]{2,1,0:T(2,128)} %bitcast.1.lists.refs_0_), channel_id=1, source_target_pairs={{0,1},{1,0},{2,3},{3,2},{4,5},{5,4},{6,7},{7,6},{8,9},{9,8},{10,11... | collective-permute-start | bytes 1160 | tf_op jit(solution)/shard_map/ppermute | solution.py:370
  5.6 2.8 %copy-start.4 = (f32[32,896]{1,0:T(8,128)S(1)}, f32[32,896]{1,0:T(8,128)}, u32[]{:S(2)}) copy-start(f32[32,896]{1,0:T(8,128)} %refs_7_.3) | copy-start | bytes 344068
  16.8 1.0 %copy-start.1 = (bf16[16,128,256]{2,1,0:T(8,128)(2,1)}, bf16[16,128,256]{2,1,0:T(8,128)(2,1)S(1)}, u32[]{:S(2)}) copy-start(bf16[16,128,256]{2,1,0:T(8,128)(2,1)S(1)} %blend.3) | copy-start | bytes 3145732
  17.7 30.5 %all-to-all-start.1 = ((bf16[16,128,256]{2,1,0:T(8,128)(2,1)}), bf16[16,128,256]{2,1,0:T(8,128)(2,1)S(1)}, u32[]{:S(2)}, u32[]{:S(2)}) async-start(bf16[16,128,256]{2,1,0:T(8,128)(2,1)} %copy-done.1), calls=%async_computation.1 | async-start | bytes 2097152 | tf_op jit(solution)/shard_map/all_to_all | solution.py:378
  33.1 1.0 %copy-start.2 = (bf16[16,120,256]{2,1,0:T(8,128)(2,1)}, bf16[16,120,256]{2,1,0:T(8,128)(2,1)S(1)}, u32[]{:S(2)}) copy-start(bf16[16,120,256]{2,1,0:T(8,128)(2,1)S(1)} %blend.2) | copy-start | bytes 2949124
  34.1 20.8 %copy-start.3 = (bf16[4,512,56]{1,2,0:T(8,128)(2,1)S(1)}, bf16[4,512,56]{1,2,0:T(8,128)(2,1)}, u32[]{:S(2)}) copy-start(bf16[4,512,56]{1,2,0:T(8,128)(2,1)} %param.9) | copy-start | bytes 688132
  48.3 28.7 %all-to-all-start = ((bf16[16,120,256]{2,1,0:T(8,128)(2,1)}), bf16[16,120,256]{2,1,0:T(8,128)(2,1)S(1)}, u32[]{:S(2)}, u32[]{:S(2)}) async-start(bf16[16,120,256]{2,1,0:T(8,128)(2,1)} %copy-done.2), calls=%async_computation | async-start | bytes 1966080 | tf_op jit(solution)/shard_map/all_to_all | solution.py:378

commit v2 on v1

--- a/solution.py
+++ b/solution.py
@@ -21,6 +21,7 @@
 CHUNKS = FIELDS // PER_CHUNK
 MID = 0.11
 VMEM = 48 * 1024 * 1024
+WHOLE_VMEM = 62 * 1024 * 1024
 
 
 def round_up(value, step):
@@ -80,22 +81,24 @@
     return pl.pallas_call(
         functools.partial(pack_kernel, z),
         out_shape=jax.ShapeDtypeStruct((z.makers - 1, z.block + z.heavy, FIELDS, FLAT), jnp.bfloat16),
-        in_specs=[pl.BlockSpec(memory_space=pltpu.SMEM), pl.BlockSpec(memory_space=pl.ANY)],
+        in_specs=[pl.BlockSpec(memory_space=pltpu.SMEM), pl.BlockSpec(memory_space=pltpu.HBM)],
         out_specs=pl.BlockSpec(memory_space=pltpu.VMEM),
         scratch_shapes=[pltpu.SemaphoreType.DMA((z.makers - 1, 1 + z.block))],
-        compiler_params=pltpu.CompilerParams(vmem_limit_bytes=VMEM),
+        compiler_params=pltpu.CompilerParams(vmem_limit_bytes=WHOLE_VMEM),
         name="pack_tiles",
     )(lists, tiles)
 
 
-def blend_kernel(z, chunk, part, *refs):
+def blend_kernel(z, chunk, place, *refs):
     lists, refs = refs[: z.makers], refs[z.makers :]
     slots = refs[: 2 * z.makers]
-    table, smoothing, out, staged, lines, turned, strength = refs[2 * z.makers :]
+    table, smoothing = refs[2 * z.makers : 2 * z.makers + 2]
+    outs, (staged, lines, turned, strength) = refs[-4 - z.regions : -4], refs[-4:]
     fields = range(chunk * PER_CHUNK, (chunk + 1) * PER_CHUNK)
     j = pl.program_id(0)
     quad = LANES // ROWS
-    region = part[0] * z.block + j
+    me = place[0]
+    region = lax.rem(me, z.makers) * z.block + j
 
     def entry(maker, slot, field):
         return lists[maker][field, slot, region]
@@ -202,32 +205,39 @@
         for f in range(PER_CHUNK):
             for t in range(TILES):
                 turned[f, LANES * t : LANES * (t + 1), :] = jnp.transpose(lines[f, t])
-        for dest in range(z.regions):
-            first = z.width * dest
-            block = [turned[f, first : first + z.span, :] for f in range(PER_CHUNK)]
-            out[dest, 0 : z.main, pl.ds(at, LANES)] = jnp.concatenate(block, 0).astype(jnp.bfloat16)
-            ends = (max(first - 1, 0), min(first + z.width, COLS - 1))
-            edge = [turned[f, end : end + 1, :] for f in range(PER_CHUNK) for end in ends]
+        for k, out in enumerate(outs):
+            dest = me ^ k
+            first = dest * z.width
+            if z.width % 8 == 0:
+                first = pl.multiple_of(first, 8)
+            block = [turned[f, pl.ds(first, z.span), :] for f in range(PER_CHUNK)]
+            out[0 : z.main, pl.ds(at, LANES)] = jnp.concatenate(block, 0).astype(jnp.bfloat16)
+            ends = (jnp.maximum(first - 1, 0), jnp.minimum(first + z.width, COLS - 1))
+            edge = [turned[f, pl.ds(end, 1), :] for f in range(PER_CHUNK) for end in ends]
             edge.append(jnp.zeros((8 - len(edge), LANES), jnp.float32))
             if chunk == 0:
                 edge.append(strength[dest, :, pl.ds(at, LANES)])
             edge = jnp.concatenate(edge, 0).astype(jnp.bfloat16)
-            out[dest, z.main : z.chunk_rows(chunk), pl.ds(at, LANES)] = edge
-
-
-def blend(z, chunk, part, lists, tiles, received, table, smoothing):
+            out[z.main : z.chunk_rows(chunk), pl.ds(at, LANES)] = edge
+
+
+def blend(z, chunk, place, lists, tiles, received, table, smoothing, earlier):
     tile_block = (1, 1, FIELDS, FLAT)
 
-    def rank(j, part, own, *others):
+    def first_region(place):
+        return lax.rem(place[0], z.makers) * z.block
+
+    def rank(j, place, own, *others):
         total = jnp.int32(0)
+        first = first_region(place)
         for before in range(z.block):
-            live = own[0, 1, part[0] * z.block + before] >= 0
+            live = own[0, 1, first + before] >= 0
             total = total + jnp.where(live & (before < j), 1, 0)
         return z.block + jnp.minimum(total, z.heavy - 1)
 
     in_specs = [
-        pl.BlockSpec(tile_block, lambda j, part, *lists: (part[0] * z.block + j, 0, 0, 0)),
-        pl.BlockSpec(tile_block, lambda j, part, *lists: (part[0] * z.block + j, 1, 0, 0)),
+        pl.BlockSpec(tile_block, lambda j, place, *lists: (first_region(place) + j, 0, 0, 0)),
+        pl.BlockSpec(tile_block, lambda j, place, *lists: (first_region(place) + j, 1, 0, 0)),
     ]
     operands = [tiles, tiles]
     for item in received:
@@ -240,15 +250,16 @@
         pl.BlockSpec(table.shape, lambda j, *scalars: (0, 0, 0)),
         pl.BlockSpec(smoothing.shape, lambda j, *scalars: (0, 0)),
     ]
-    shape = (z.regions, z.chunk_rows(chunk), z.part)
+    in_specs += [pl.BlockSpec(memory_space=pl.ANY)] * len(earlier)
+    shape = (z.chunk_rows(chunk), z.part)
     return pl.pallas_call(
         functools.partial(blend_kernel, z, chunk),
-        out_shape=jax.ShapeDtypeStruct(shape, jnp.bfloat16),
+        out_shape=[jax.ShapeDtypeStruct(shape, jnp.bfloat16)] * z.regions,
         grid_spec=pltpu.PrefetchScalarGridSpec(
             num_scalar_prefetch=1 + z.makers,
             grid=(z.block,),
             in_specs=in_specs,
-            out_specs=pl.BlockSpec(shape, lambda j, *scalars: (0, 0, 0)),
+            out_specs=[pl.BlockSpec(shape, lambda j, *scalars: (0, 0))] * z.regions,
             scratch_shapes=[
                 pltpu.VMEM((2 * z.makers, TILES, PAIRS * FIELDS, LANES), jnp.float32),
                 pltpu.VMEM((PER_CHUNK, TILES, LANES, LANES), jnp.float32),
@@ -259,7 +270,7 @@
         compiler_params=pltpu.CompilerParams(vmem_limit_bytes=VMEM),
         cost_estimate=pl.CostEstimate(flops=50_000_000, bytes_accessed=4_000_000, transcendentals=0),
         name="blend",
-    )(part, *lists, *operands, table, smoothing)
+    )(place, *lists, *operands, table, smoothing, *earlier)
 
 
 SORT_STEPS = (
@@ -272,25 +283,39 @@
 )
 
 
-def score_kernel(z, chunk, block, strength_block, analysis, *refs):
-    crps, spread = refs[-6:-4]
-    strength, padded, members, results = refs[-4:]
+def score_kernel(z, chunk, place, *refs):
+    blocks, refs = refs[: z.regions], refs[z.regions :]
+    me = place[0]
+    if chunk == 0:
+        analysis, crps, spread, strength, padded, members, results = refs
+        slot = lax.broadcasted_iota(jnp.int32, (8, LANES), 1) // ROWS
+        quad = LANES // ROWS
+        for first in range(0, z.regions, quad):
+            pieces = []
+            for k in range(first, first + quad):
+                piece = blocks[k][z.main : z.main + 16, :].astype(jnp.float32)[8:16]
+                turn = lax.rem(me ^ k, quad)
+                pieces.append((pltpu.roll(piece, turn * ROWS, 1), turn))
+            at = pl.multiple_of(lax.div(me ^ first, quad) * LANES, LANES)
+            for g in range(z.span // 8):
+                joined = jnp.full((8, LANES), MID)
+                for piece, turn in pieces:
+                    near = pltpu.roll(piece, (z.part - ROWS * g) % z.part, 1)[:, :LANES]
+                    joined = jnp.where(slot == turn, near + MID, joined)
+                strength[8 * g : 8 * (g + 1), pl.ds(at, LANES)] = joined
+    else:
+        strength, analysis = refs[:2]
+        crps, spread, padded, members, results = refs[-5:]
     rows = z.rows
-    for source in range(z.regions):
-        piece = strength_block[source].astype(jnp.float32)[8:16]
-        for g in range(z.span // 8):
-            strength[8 * g : 8 * (g + 1), ROWS * source : ROWS * (source + 1)] = (
-                piece[:, ROWS * g : ROWS * (g + 1)] + MID
-            )
     lane = lax.broadcasted_iota(jnp.int32, (8, rows), 1)
     for f in range(PER_CHUNK):
         for sample in range(SAMPLES):
-            for part in range(z.makers):
-                source = sample * z.makers + part
-                lanes = slice(part * z.part, (part + 1) * z.part)
-                values = block[source, 0 : z.main, :].astype(jnp.float32)
+            for k in range(sample * z.makers, (sample + 1) * z.makers):
+                block = blocks[k]
+                lanes = pl.ds(pl.multiple_of(lax.rem(me ^ k, z.makers) * z.part, LANES), z.part)
+                values = block[0 : z.main, :].astype(jnp.float32)
                 padded[8 : 8 + z.span, lanes] = values[f * z.span : (f + 1) * z.span]
-                edge = block[source, z.main : z.main + 8, :].astype(jnp.float32)
+                edge = block[z.main : z.main + 8, :].astype(jnp.float32)
                 padded[7:8, lanes] = edge[2 * f : 2 * f + 1]
                 padded[8 + z.width : 9 + z.width, lanes] = edge[2 * f + 1 : 2 * f + 2]
             for g in range(z.span // 8):
@@ -326,43 +351,59 @@
         spread[1, f] = results[2, 0 : z.width, :].astype(jnp.bfloat16)
 
 
-def score(z, chunk, block, first_block, analysis, earlier):
+def score(z, chunk, place, blocks, analysis, strength, earlier):
     width, rows = z.width, z.rows
-    tail = z.main // 16
-    in_specs = [
-        pl.BlockSpec(block.shape, lambda i: (0, 0, 0)),
-        pl.BlockSpec((z.regions, 16, z.part), lambda i: (0, tail, 0)),
-        pl.BlockSpec((PER_CHUNK, width, rows), lambda i: (chunk, 0, 0)),
+    in_specs = [pl.BlockSpec(blocks[0].shape, lambda i, place: (0, 0))] * z.regions
+    if chunk:
+        in_specs.append(pl.BlockSpec(strength.shape, lambda i, place: (0, 0)))
+    in_specs.append(pl.BlockSpec((PER_CHUNK, width, rows), lambda i, place: (chunk, 0, 0)))
+    in_specs += [pl.BlockSpec(memory_space=pl.ANY)] * len(earlier)
+    out_shape = [
+        jax.ShapeDtypeStruct((FIELDS, width, rows), jnp.bfloat16),
+        jax.ShapeDtypeStruct((2, FIELDS, width, rows), jnp.bfloat16),
     ]
-    in_specs += [pl.BlockSpec(memory_space=pl.ANY)] * len(earlier)
+    out_specs = [
+        pl.BlockSpec((PER_CHUNK, width, rows), lambda i, place: (chunk, 0, 0)),
+        pl.BlockSpec((2, PER_CHUNK, width, rows), lambda i, place: (0, chunk, 0, 0)),
+    ]
+    if chunk == 0:
+        out_shape.append(jax.ShapeDtypeStruct((z.span, rows), jnp.float32))
+        out_specs.append(pl.BlockSpec((z.span, rows), lambda i, place: (0, 0)))
+    operands = [place, *blocks, *([strength] if chunk else []), analysis]
     return pl.pallas_call(
         functools.partial(score_kernel, z, chunk),
-        out_shape=[
-            jax.ShapeDtypeStruct((FIELDS, width, rows), jnp.bfloat16),
-            jax.ShapeDtypeStruct((2, FIELDS, width, rows), jnp.bfloat16),
-        ],
-        grid=(1,),
-        in_specs=in_specs,
-        out_specs=[
-            pl.BlockSpec((PER_CHUNK, width, rows), lambda i: (chunk, 0, 0)),
-            pl.BlockSpec((2, PER_CHUNK, width, rows), lambda i: (0, chunk, 0, 0)),
-        ],
-        scratch_shapes=[
-            pltpu.VMEM((z.span, rows), jnp.float32),
-            pltpu.VMEM((z.span + 16, rows), jnp.float32),
-            pltpu.VMEM((SAMPLES, z.span, rows), jnp.float32),
-            pltpu.VMEM((3, z.span, rows), jnp.float32),
-        ],
-        input_output_aliases={3 + i: i for i in range(len(earlier))},
+        out_shape=out_shape,
+        grid_spec=pltpu.PrefetchScalarGridSpec(
+            num_scalar_prefetch=1,
+            grid=(1,),
+            in_specs=in_specs,
+            out_specs=out_specs,
+            scratch_shapes=[
+                pltpu.VMEM((z.span + 16, rows), jnp.float32),
+                pltpu.VMEM((SAMPLES, z.span, rows), jnp.float32),
+                pltpu.VMEM((3, z.span, rows), jnp.float32),
+            ],
+        ),
+        input_output_aliases={len(operands) + i: i for i in range(len(earlier))},
         compiler_params=pltpu.CompilerParams(vmem_limit_bytes=VMEM),
         cost_estimate=pl.CostEstimate(flops=30_000_000, bytes_accessed=3_000_000, transcendentals=0),
         name="score",
-    )(block, first_block, analysis, *earlier)
+    )(*operands, *earlier)
+
+
+def swap_order(regions):
+    far, near = list(range(regions // 2, regions)), list(range(regions // 2 - 1, 0, -1))
+    order = []
+    while far or near:
+        taken = 1 if far else len(near)
+        order += far[:2] + near[:taken]
+        far, near = far[2:], near[taken:]
+    return order
 
 
 def shards(patch_tiles, slot_lists, blend_table, smoothing, analysis):
     z = Sizes(lax.axis_size("region"))
-    part = lax.rem(lax.axis_index("region"), z.makers)
+    place = lax.axis_index("region").reshape(1)
     turns = [
         [(i, i - i % z.makers + (i + k) % z.makers) for i in range(z.regions)] for k in range(1, z.makers)
     ]
@@ -371,15 +412,19 @@
     packed = pack_tiles(z, lists[0], patch_tiles)
     received = [lax.ppermute(packed[k : k + 1], "region", turn) for k, turn in enumerate(turns)]
     table = blend_table.reshape(blend_table.shape[0], PAIRS, COLS)
-    blocks = [
-        blend(z, chunk, part.reshape(1), lists, patch_tiles, received, table, smoothing)
-        for chunk in range(CHUNKS)
-    ]
-    moved = [lax.all_to_all(item, "region", split_axis=0, concat_axis=0, tiled=True) for item in blocks]
+    arrived = []
+    for chunk in range(CHUNKS):
+        earlier = [blocks[0] for blocks in arrived]
+        blocks = list(blend(z, chunk, place, lists, patch_tiles, received, table, smoothing, earlier))
+        for k in swap_order(z.regions):
+            blocks[k] = lax.ppermute(blocks[k], "region", [(i, i ^ k) for i in range(z.regions)])
+        arrived.append(blocks)
     analysis = jnp.swapaxes(analysis, 1, 2)
-    outs = ()
+    strength, outs = None, ()
     for chunk in range(CHUNKS):
-        outs = score(z, chunk, moved[chunk], moved[0], analysis, outs)
+        outs = score(z, chunk, place, arrived[chunk], analysis, strength, outs)
+        if chunk == 0:
+            strength, outs = outs[2], outs[:2]
     return tuple(jnp.swapaxes(item, -1, -2) for item in outs)
 
 

time: 81.7 us -> 91 us (1.11); the launches traced: 80.2 us -> 91.5 us
  starting transfers between devices: 14.6 us -> 55 us
  waiting for transfers between devices: 35.4 us -> 7.71 us
  local copies, waits for them, and re-layouts: 4.23 us -> 1.46 us
  Pallas kernels: 25.2 us -> 26.6 us
    ppermute x0 -> x30, starting transfers between devices: none -> 54.4 us  [shards(): lax.ppermute(blocks[k], 'region', [(i, i ^ k) for i in range(z.regions)])]
    all_to_all x2 -> x0, waiting for transfers between devices: 32.8 us -> none  [shards(): lax.all_to_all(item, 'region', split_axis=0, concat_axis=0, tiled=True)]
    all_to_all x2 -> x0, starting transfers between devices: 14.1 us -> none  [shards(): lax.all_to_all(item, 'region', split_axis=0, concat_axis=0, tiled=True)]
    ppermute x0 -> x30, waiting for transfers between devices: none -> 6.33 us  [shards(): lax.ppermute(blocks[k], 'region', [(i, i ^ k) for i in range(z.regions)])]
    unnamed x13 -> x7, local copies, waits for them, and re-layouts: 4.17 us -> 1.41 us
    ppermute x1, waiting for transfers between devices: 2.58 us -> 0.85 us  [shards(): lists = [lists] + [lax.ppermute(lists, 'region', turn) for turn in turns]]
  transfers between devices with their start and end apart: 4 -> 32, of which waited for: 3 -> 6; matrix products, arithmetic and copies ran while one was open for 0% -> 2% of each run, Pallas kernels for 14% -> 4%
where the time goes in v2:
time: 91 us; the launch traced here: 91.5 us
  starting transfers between devices  55 us (60%)
  Pallas kernels  26.6 us (29%)
  waiting for transfers between devices  7.71 us (8%)
  local copies, waits for them, and re-layouts  1.46 us (2%)
    ppermute x30, starting transfers between devices, shards(): lax.ppermute(blocks[k], 'region', [(i, i ^ k) for i in range(z.regions)])  54.4 us
    pallas_call x2, Pallas kernels, blend(): pl.pallas_call(functools.partial(blend_kernel, z, chunk), out_shape=[jax....  16.4 us
    pallas_call x2, Pallas kernels, score(): pl.pallas_call(functools.partial(score_kernel, z, chunk), out_shape=out_s...  6.89 us
    ppermute x30, waiting for transfers between devices, shards(): lax.ppermute(blocks[k], 'region', [(i, i ^ k) for i in range(z.regions)])  6.33 us
    pallas_call x1, Pallas kernels, pack_tiles(): pl.pallas_call(functools.partial(pack_kernel, z), out_shape=jax.ShapeDtyp...  3.26 us
  transfers between devices with their start and end apart: 32, of which 6 were waited for; matrix products, arithmetic and copies ran while one was open for 2% of the time, Pallas kernels for 4%

profile of v2, /device:TPU:1, one launch (start us, length us, event | category | flops | bytes accessed | tf_op | source)
XLA Modules:
  0.0 91.5 jit_solution(115540354107347782)
XLA Ops:
  0.6 3.3 %pack_tiles.1 = bf16[1,12,4,14336]{3,2,1,0:T(4,128)(2,1)} custom-call(s32[3,2,16]{2,1,0:T(2,128)} %bitcast.10, bf16[16,2,4,14336]{3,2,1,0:T(4,128)(2,1)} %refs_3_.3), custom_call_target="tpu_custom_call" | custom-call | tf_op jit(solution)/shard_map/pack_tiles/pallas_call | solution.py:81
  4.5 1.4 %copy.9 = f32[2,8,16,896]{3,2,1,0:T(8,128)S(1)} copy(f32[2,8,16,896]{3,1,2,0:T(8,128)} %bitcast.15) | data formatting | bytes 1835008
  7.3 8.4 %blend.2 = (bf16[128,256]{1,0:T(8,128)(2,1)S(1)}, bf16[128,256]{1,0:T(8,128)(2,1)S(1)}, bf16[128,256]{1,0:T(8,128)(2,1)S(1)}, bf16[128,256]{1,0:T(8,128)(2,1)S(1...) custom-call(s32[1]{0:T(128)} %bitcast.place, ...), custom_call_target="tpu_custom_call" | custom-call | flops 50000000 | bytes 4000000 | tf_op jit(solution)/shard_map/blend/pallas_call | solution.py:255
  15.7 8.1 %blend.3 = (bf16[120,256]{1,0:T(8,128)(2,1)S(1)}, bf16[120,256]{1,0:T(8,128)(2,1)S(1)}, bf16[120,256]{1,0:T(8,128)(2,1)S(1)}, bf16[120,256]{1,0:T(8,128)(2,1)S(1...) custom-call(s32[1]{0:T(128)} %bitcast.place, ...), custom_call_target="tpu_custom_call" | custom-call | flops 50000000 | bytes 4000000 | tf_op jit(solution)/shard_map/blend/pallas_call | solution.py:255
  23.8 3.8 %collective-permute-start.10 = (bf16[120,256]{1,0:T(8,128)(2,1)S(1)}, bf16[120,256]{1,0:T(8,128)(2,1)S(1)}, u32[]{:S(2)}, u32[]{:S(2)}) collective-permute-start(bf16[120,256]{1,0:T(8,128)(2,1)S(1)} %get-tuple-element.49), channel_id=1, source_target_pairs={{0,9},{1,8},{2,11},{3,10},{4,13},{5,12},{6,15},{7,14},{8,1},{9,0},... | collective-permute-start | bytes 184328 | tf_op jit(solution)/shard_map/ppermute | solution.py:420
  28.5 2.6 %collective-permute-start.12 = (bf16[120,256]{1,0:T(8,128)(2,1)S(1)}, bf16[120,256]{1,0:T(8,128)(2,1)S(1)}, u32[]{:S(2)}, u32[]{:S(2)}) collective-permute-start(bf16[120,256]{1,0:T(8,128)(2,1)S(1)} %get-tuple-element.51), channel_id=1, source_target_pairs={{0,11},{1,10},{2,9},{3,8},{4,15},{5,14},{6,13},{7,12},{8,3},{9,2},... | collective-permute-start | bytes 184328 | tf_op jit(solution)/shard_map/ppermute | solution.py:420
  32.2 2.4 %collective-permute-start.14 = (bf16[120,256]{1,0:T(8,128)(2,1)S(1)}, bf16[120,256]{1,0:T(8,128)(2,1)S(1)}, u32[]{:S(2)}, u32[]{:S(2)}) collective-permute-start(bf16[120,256]{1,0:T(8,128)(2,1)S(1)} %get-tuple-element.53), channel_id=1, source_target_pairs={{0,13},{1,12},{2,15},{3,14},{4,9},{5,8},{6,11},{7,10},{8,5},{9,4},... | collective-permute-start | bytes 184328 | tf_op jit(solution)/shard_map/ppermute | solution.py:420
  34.6 5.0 %collective-permute-start.15 = (bf16[120,256]{1,0:T(8,128)(2,1)S(1)}, bf16[120,256]{1,0:T(8,128)(2,1)S(1)}, u32[]{:S(2)}, u32[]{:S(2)}) collective-permute-start(bf16[120,256]{1,0:T(8,128)(2,1)S(1)} %get-tuple-element.54), channel_id=1, source_target_pairs={{0,14},{1,15},{2,12},{3,13},{4,10},{5,11},{6,8},{7,9},{8,6},{9,7},... | collective-permute-start | bytes 184328 | tf_op jit(solution)/shard_map/ppermute | solution.py:420
  39.6 2.9 %collective-permute-start.16 = (bf16[120,256]{1,0:T(8,128)(2,1)S(1)}, bf16[120,256]{1,0:T(8,128)(2,1)S(1)}, u32[]{:S(2)}, u32[]{:S(2)}) collective-permute-start(bf16[120,256]{1,0:T(8,128)(2,1)S(1)} %get-tuple-element.55), channel_id=1, source_target_pairs={{0,15},{1,14},{2,13},{3,12},{4,11},{5,10},{6,9},{7,8},{8,7},{9,6},... | collective-permute-start | bytes 184328 | tf_op jit(solution)/shard_map/ppermute | solution.py:420
  44.6 2.2 %collective-permute-done.16.refs_15_ = bf16[120,256]{1,0:T(8,128)(2,1)S(1)} collective-permute-done((bf16[120,256]{1,0:T(8,128)(2,1)S(1)}, bf16[120,256]{1,0:T(8,128)(2,1)S(1)}, u32[]{:S(2)}, u32[]{:S(2)}) %collective-permute-start.16) | collective-permute-done | bytes 61472 | tf_op jit(solution)/shard_map/ppermute | solution.py:420
  46.8 2.1 %collective-permute-start.19 = (bf16[128,256]{1,0:T(8,128)(2,1)S(1)}, bf16[128,256]{1,0:T(8,128)(2,1)S(1)}, u32[]{:S(2)}, u32[]{:S(2)}) collective-permute-start(bf16[128,256]{1,0:T(8,128)(2,1)S(1)} %get-tuple-element.58), channel_id=1, source_target_pairs={{0,3},{1,2},{2,1},{3,0},{4,7},{5,6},{6,5},{7,4},{8,11},{9,10},{10,... | collective-permute-start | bytes 196616 | tf_op jit(solution)/shard_map/ppermute | solution.py:420
  48.9 1.5 %collective-permute-start.20 = (bf16[128,256]{1,0:T(8,128)(2,1)S(1)}, bf16[128,256]{1,0:T(8,128)(2,1)S(1)}, u32[]{:S(2)}, u32[]{:S(2)}) collective-permute-start(bf16[128,256]{1,0:T(8,128)(2,1)S(1)} %get-tuple-element.59), channel_id=1, source_target_pairs={{0,4},{1,5},{2,6},{3,7},{4,0},{5,1},{6,2},{7,3},{8,12},{9,13},{10,... | collective-permute-start | bytes 196616 | tf_op jit(solution)/shard_map/ppermute | solution.py:420
  50.4 2.0 %collective-permute-start.22 = (bf16[128,256]{1,0:T(8,128)(2,1)S(1)}, bf16[128,256]{1,0:T(8,128)(2,1)S(1)}, u32[]{:S(2)}, u32[]{:S(2)}) collective-permute-start(bf16[128,256]{1,0:T(8,128)(2,1)S(1)} %get-tuple-element.61), channel_id=1, source_target_pairs={{0,6},{1,7},{2,4},{3,5},{4,2},{5,3},{6,0},{7,1},{8,14},{9,15},{10,... | collective-permute-start | bytes 196616 | tf_op jit(solution)/shard_map/ppermute | solution.py:420
  53.5 3.5 %collective-permute-start.24 = (bf16[128,256]{1,0:T(8,128)(2,1)S(1)}, bf16[128,256]{1,0:T(8,128)(2,1)S(1)}, u32[]{:S(2)}, u32[]{:S(2)}) collective-permute-start(bf16[128,256]{1,0:T(8,128)(2,1)S(1)} %get-tuple-element.63), channel_id=1, source_target_pairs={{0,8},{1,9},{2,10},{3,11},{4,12},{5,13},{6,14},{7,15},{8,0},{9,1},... | collective-permute-start | bytes 196616 | tf_op jit(solution)/shard_map/ppermute | solution.py:420
  57.2 2.2 %collective-permute-start.26 = (bf16[128,256]{1,0:T(8,128)(2,1)S(1)}, bf16[128,256]{1,0:T(8,128)(2,1)S(1)}, u32[]{:S(2)}, u32[]{:S(2)}) collective-permute-start(bf16[128,256]{1,0:T(8,128)(2,1)S(1)} %get-tuple-element.65), channel_id=1, source_target_pairs={{0,10},{1,11},{2,8},{3,9},{4,14},{5,15},{6,12},{7,13},{8,2},{9,3},... | collective-permute-start | bytes 196616 | tf_op jit(solution)/shard_map/ppermute | solution.py:420
  59.5 1.5 %collective-permute-start.27 = (bf16[128,256]{1,0:T(8,128)(2,1)S(1)}, bf16[128,256]{1,0:T(8,128)(2,1)S(1)}, u32[]{:S(2)}, u32[]{:S(2)}) collective-permute-start(bf16[128,256]{1,0:T(8,128)(2,1)S(1)} %get-tuple-element.66), channel_id=1, source_target_pairs={{0,11},{1,10},{2,9},{3,8},{4,15},{5,14},{6,13},{7,12},{8,3},{9,2},... | collective-permute-start | bytes 196616 | tf_op jit(solution)/shard_map/ppermute | solution.py:420
  60.9 2.1 %collective-permute-start.28 = (bf16[128,256]{1,0:T(8,128)(2,1)S(1)}, bf16[128,256]{1,0:T(8,128)(2,1)S(1)}, u32[]{:S(2)}, u32[]{:S(2)}) collective-permute-start(bf16[128,256]{1,0:T(8,128)(2,1)S(1)} %get-tuple-element.67), channel_id=1, source_target_pairs={{0,12},{1,13},{2,14},{3,15},{4,8},{5,9},{6,10},{7,11},{8,4},{9,5},... | collective-permute-start | bytes 196616 | tf_op jit(solution)/shard_map/ppermute | solution.py:420
  63.1 6.4 %collective-permute-start.29 = (bf16[128,256]{1,0:T(8,128)(2,1)S(1)}, bf16[128,256]{1,0:T(8,128)(2,1)S(1)}, u32[]{:S(2)}, u32[]{:S(2)}) collective-permute-start(bf16[128,256]{1,0:T(8,128)(2,1)S(1)} %get-tuple-element.68), channel_id=1, source_target_pairs={{0,13},{1,12},{2,15},{3,14},{4,9},{5,8},{6,11},{7,10},{8,5},{9,4},... | collective-permute-start | bytes 196616 | tf_op jit(solution)/shard_map/ppermute | solution.py:420
  71.7 2.4 %collective-permute-start.31 = (bf16[128,256]{1,0:T(8,128)(2,1)S(1)}, bf16[128,256]{1,0:T(8,128)(2,1)S(1)}, u32[]{:S(2)}, u32[]{:S(2)}) collective-permute-start(bf16[128,256]{1,0:T(8,128)(2,1)S(1)} %get-tuple-element.70), channel_id=1, source_target_pairs={{0,15},{1,14},{2,13},{3,12},{4,11},{5,10},{6,9},{7,8},{8,7},{9,6},... | collective-permute-start | bytes 196616 | tf_op jit(solution)/shard_map/ppermute | solution.py:420
  74.1 2.7 %collective-permute-start.6 = (bf16[120,256]{1,0:T(8,128)(2,1)S(1)}, bf16[120,256]{1,0:T(8,128)(2,1)S(1)}, u32[]{:S(2)}, u32[]{:S(2)}) collective-permute-start(bf16[120,256]{1,0:T(8,128)(2,1)S(1)} %get-tuple-element.45), channel_id=1, source_target_pairs={{0,5},{1,4},{2,7},{3,6},{4,1},{5,0},{6,3},{7,2},{8,13},{9,12},{10,... | collective-permute-start | bytes 184328 | tf_op jit(solution)/shard_map/ppermute | solution.py:420
  78.1 3.8 %collective-permute-start.8 = (bf16[120,256]{1,0:T(8,128)(2,1)S(1)}, bf16[120,256]{1,0:T(8,128)(2,1)S(1)}, u32[]{:S(2)}, u32[]{:S(2)}) collective-permute-start(bf16[120,256]{1,0:T(8,128)(2,1)S(1)} %get-tuple-element.47), channel_id=1, source_target_pairs={{0,7},{1,6},{2,5},{3,4},{4,3},{5,2},{6,1},{7,0},{8,15},{9,14},{10,... | collective-permute-start | bytes 184328 | tf_op jit(solution)/shard_map/ppermute | solution.py:420
  82.2 3.5 %score.2 = (bf16[4,56,512]{2,1,0:T(8,128)(2,1)}, bf16[2,4,56,512]{3,2,1,0:T(8,128)(2,1)}, f32[56,512]{1,0:T(8,128)S(1)}) custom-call(s32[1]{0:T(128)} %bitcast.place, bf16[128,256]{1,0:T(8,128)(2,1)S(1)} %get-tuple-element.39.refs_8_.refs_0_, bf16[128,256]{1,0:T(8,128)(2,1)S(1)} %collective-permute-done.17.refs_1_, ...), custom_call_target="tpu_custom_call" | custom-call | flops 30000000 | bytes 3000000 | tf_op jit(solution)/shard_map/score/pallas_call | solution.py:373
  85.7 2.4 %collective-permute-done.9.refs_8_ = bf16[120,256]{1,0:T(8,128)(2,1)S(1)} collective-permute-done((bf16[120,256]{1,0:T(8,128)(2,1)S(1)}, bf16[120,256]{1,0:T(8,128)(2,1)S(1)}, u32[]{:S(2)}, u32[]{:S(2)}) %collective-permute-start.9) | collective-permute-done | bytes 61472 | tf_op jit(solution)/shard_map/ppermute | solution.py:420
  88.1 3.4 %score.3 = (bf16[4,56,512]{2,1,0:T(8,128)(2,1)}, bf16[2,4,56,512]{3,2,1,0:T(8,128)(2,1)}) custom-call(s32[1]{0:T(128)} %bitcast.place, bf16[120,256]{1,0:T(8,128)(2,1)S(1)} %get-tuple-element.40.refs_0_, bf16[120,256]{1,0:T(8,128)(2,1)S(1)} %collective-permute-done.2.refs_1_, ...), custom_call_target="tpu_custom_call", output_to_operand_aliasing={{0}: (19, {}), {1}: (20, {})} | custom-call | flops 30000000 | bytes 3000000 | tf_op jit(solution)/shard_map/score/pallas_call | solution.py:373
  (53 shorter events, 11.5 us)
Async XLA Ops:
  23.8 10.8 %collective-permute-start.10 = (bf16[120,256]{1,0:T(8,128)(2,1)S(1)}, bf16[120,256]{1,0:T(8,128)(2,1)S(1)}, u32[]{:S(2)}, u32[]{:S(2)}) collective-permute-start(bf16[120,256]{1,0:T(8,128)(2,1)S(1)} %get-tuple-element.49), channel_id=1, source_target_pairs={{0,9},{1,8},{2,11},{3,10},{4,13},{5,12},{6,15},{7,14},{8,1},{9,0},... | collective-permute-start | bytes 184328 | tf_op jit(solution)/shard_map/ppermute | solution.py:420
  27.5 12.1 %collective-permute-start.11 = (bf16[120,256]{1,0:T(8,128)(2,1)S(1)}, bf16[120,256]{1,0:T(8,128)(2,1)S(1)}, u32[]{:S(2)}, u32[]{:S(2)}) collective-permute-start(bf16[120,256]{1,0:T(8,128)(2,1)S(1)} %get-tuple-element.50), channel_id=1, source_target_pairs={{0,10},{1,11},{2,8},{3,9},{4,14},{5,15},{6,12},{7,13},{8,2},{9,3},... | collective-permute-start | bytes 184328 | tf_op jit(solution)/shard_map/ppermute | solution.py:420
  28.5 13.9 %collective-permute-start.12 = (bf16[120,256]{1,0:T(8,128)(2,1)S(1)}, bf16[120,256]{1,0:T(8,128)(2,1)S(1)}, u32[]{:S(2)}, u32[]{:S(2)}) collective-permute-start(bf16[120,256]{1,0:T(8,128)(2,1)S(1)} %get-tuple-element.51), channel_id=1, source_target_pairs={{0,11},{1,10},{2,9},{3,8},{4,15},{5,14},{6,13},{7,12},{8,3},{9,2},... | collective-permute-start | bytes 184328 | tf_op jit(solution)/shard_map/ppermute | solution.py:420
  31.1 11.4 %collective-permute-start.13 = (bf16[120,256]{1,0:T(8,128)(2,1)S(1)}, bf16[120,256]{1,0:T(8,128)(2,1)S(1)}, u32[]{:S(2)}, u32[]{:S(2)}) collective-permute-start(bf16[120,256]{1,0:T(8,128)(2,1)S(1)} %get-tuple-element.52), channel_id=1, source_target_pairs={{0,12},{1,13},{2,14},{3,15},{4,8},{5,9},{6,10},{7,11},{8,4},{9,5},... | collective-permute-start | bytes 184328 | tf_op jit(solution)/shard_map/ppermute | solution.py:420
  32.2 11.6 %collective-permute-start.14 = (bf16[120,256]{1,0:T(8,128)(2,1)S(1)}, bf16[120,256]{1,0:T(8,128)(2,1)S(1)}, u32[]{:S(2)}, u32[]{:S(2)}) collective-permute-start(bf16[120,256]{1,0:T(8,128)(2,1)S(1)} %get-tuple-element.53), channel_id=1, source_target_pairs={{0,13},{1,12},{2,15},{3,14},{4,9},{5,8},{6,11},{7,10},{8,5},{9,4},... | collective-permute-start | bytes 184328 | tf_op jit(solution)/shard_map/ppermute | solution.py:420
  34.6 10.0 %collective-permute-start.15 = (bf16[120,256]{1,0:T(8,128)(2,1)S(1)}, bf16[120,256]{1,0:T(8,128)(2,1)S(1)}, u32[]{:S(2)}, u32[]{:S(2)}) collective-permute-start(bf16[120,256]{1,0:T(8,128)(2,1)S(1)} %get-tuple-element.54), channel_id=1, source_target_pairs={{0,14},{1,15},{2,12},{3,13},{4,10},{5,11},{6,8},{7,9},{8,6},{9,7},... | collective-permute-start | bytes 184328 | tf_op jit(solution)/shard_map/ppermute | solution.py:420
  39.6 7.2 %collective-permute-start.16 = (bf16[120,256]{1,0:T(8,128)(2,1)S(1)}, bf16[120,256]{1,0:T(8,128)(2,1)S(1)}, u32[]{:S(2)}, u32[]{:S(2)}) collective-permute-start(bf16[120,256]{1,0:T(8,128)(2,1)S(1)} %get-tuple-element.55), channel_id=1, source_target_pairs={{0,15},{1,14},{2,13},{3,12},{4,11},{5,10},{6,9},{7,8},{8,7},{9,6},... | collective-permute-start | bytes 184328 | tf_op jit(solution)/shard_map/ppermute | solution.py:420
  46.8 6.7 %collective-permute-start.19 = (bf16[128,256]{1,0:T(8,128)(2,1)S(1)}, bf16[128,256]{1,0:T(8,128)(2,1)S(1)}, u32[]{:S(2)}, u32[]{:S(2)}) collective-permute-start(bf16[128,256]{1,0:T(8,128)(2,1)S(1)} %get-tuple-element.58), channel_id=1, source_target_pairs={{0,3},{1,2},{2,1},{3,0},{4,7},{5,6},{6,5},{7,4},{8,11},{9,10},{10,... | collective-permute-start | bytes 196616 | tf_op jit(solution)/shard_map/ppermute | solution.py:420
  48.9 8.1 %collective-permute-start.20 = (bf16[128,256]{1,0:T(8,128)(2,1)S(1)}, bf16[128,256]{1,0:T(8,128)(2,1)S(1)}, u32[]{:S(2)}, u32[]{:S(2)}) collective-permute-start(bf16[128,256]{1,0:T(8,128)(2,1)S(1)} %get-tuple-element.59), channel_id=1, source_target_pairs={{0,4},{1,5},{2,6},{3,7},{4,0},{5,1},{6,2},{7,3},{8,12},{9,13},{10,... | collective-permute-start | bytes 196616 | tf_op jit(solution)/shard_map/ppermute | solution.py:420
  50.4 6.8 %collective-permute-start.21 = (bf16[128,256]{1,0:T(8,128)(2,1)S(1)}, bf16[128,256]{1,0:T(8,128)(2,1)S(1)}, u32[]{:S(2)}, u32[]{:S(2)}) collective-permute-start(bf16[128,256]{1,0:T(8,128)(2,1)S(1)} %get-tuple-element.60), channel_id=1, source_target_pairs={{0,5},{1,4},{2,7},{3,6},{4,1},{5,0},{6,3},{7,2},{8,13},{9,12},{10,... | collective-permute-start | bytes 196616 | tf_op jit(solution)/shard_map/ppermute | solution.py:420
  50.4 9.1 %collective-permute-start.22 = (bf16[128,256]{1,0:T(8,128)(2,1)S(1)}, bf16[128,256]{1,0:T(8,128)(2,1)S(1)}, u32[]{:S(2)}, u32[]{:S(2)}) collective-permute-start(bf16[128,256]{1,0:T(8,128)(2,1)S(1)} %get-tuple-element.61), channel_id=1, source_target_pairs={{0,6},{1,7},{2,4},{3,5},{4,2},{5,3},{6,0},{7,1},{8,14},{9,15},{10,... | collective-permute-start | bytes 196616 | tf_op jit(solution)/shard_map/ppermute | solution.py:420
  52.4 8.5 %collective-permute-start.23 = (bf16[128,256]{1,0:T(8,128)(2,1)S(1)}, bf16[128,256]{1,0:T(8,128)(2,1)S(1)}, u32[]{:S(2)}, u32[]{:S(2)}) collective-permute-start(bf16[128,256]{1,0:T(8,128)(2,1)S(1)} %get-tuple-element.62), channel_id=1, source_target_pairs={{0,7},{1,6},{2,5},{3,4},{4,3},{5,2},{6,1},{7,0},{8,15},{9,14},{10,... | collective-permute-start | bytes 196616 | tf_op jit(solution)/shard_map/ppermute | solution.py:420
  53.5 9.5 %collective-permute-start.24 = (bf16[128,256]{1,0:T(8,128)(2,1)S(1)}, bf16[128,256]{1,0:T(8,128)(2,1)S(1)}, u32[]{:S(2)}, u32[]{:S(2)}) collective-permute-start(bf16[128,256]{1,0:T(8,128)(2,1)S(1)} %get-tuple-element.63), channel_id=1, source_target_pairs={{0,8},{1,9},{2,10},{3,11},{4,12},{5,13},{6,14},{7,15},{8,0},{9,1},... | collective-permute-start | bytes 196616 | tf_op jit(solution)/shard_map/ppermute | solution.py:420
  57.0 12.9 %collective-permute-start.25 = (bf16[128,256]{1,0:T(8,128)(2,1)S(1)}, bf16[128,256]{1,0:T(8,128)(2,1)S(1)}, u32[]{:S(2)}, u32[]{:S(2)}) collective-permute-start(bf16[128,256]{1,0:T(8,128)(2,1)S(1)} %get-tuple-element.64), channel_id=1, source_target_pairs={{0,9},{1,8},{2,11},{3,10},{4,13},{5,12},{6,15},{7,14},{8,1},{9,0},... | collective-permute-start | bytes 196616 | tf_op jit(solution)/shard_map/ppermute | solution.py:420
  57.2 14.5 %collective-permute-start.26 = (bf16[128,256]{1,0:T(8,128)(2,1)S(1)}, bf16[128,256]{1,0:T(8,128)(2,1)S(1)}, u32[]{:S(2)}, u32[]{:S(2)}) collective-permute-start(bf16[128,256]{1,0:T(8,128)(2,1)S(1)} %get-tuple-element.65), channel_id=1, source_target_pairs={{0,10},{1,11},{2,8},{3,9},{4,14},{5,15},{6,12},{7,13},{8,2},{9,3},... | collective-permute-start | bytes 196616 | tf_op jit(solution)/shard_map/ppermute | solution.py:420
  59.5 14.6 %collective-permute-start.27 = (bf16[128,256]{1,0:T(8,128)(2,1)S(1)}, bf16[128,256]{1,0:T(8,128)(2,1)S(1)}, u32[]{:S(2)}, u32[]{:S(2)}) collective-permute-start(bf16[128,256]{1,0:T(8,128)(2,1)S(1)} %get-tuple-element.66), channel_id=1, source_target_pairs={{0,11},{1,10},{2,9},{3,8},{4,15},{5,14},{6,13},{7,12},{8,3},{9,2},... | collective-permute-start | bytes 196616 | tf_op jit(solution)/shard_map/ppermute | solution.py:420
  60.9 13.2 %collective-permute-start.28 = (bf16[128,256]{1,0:T(8,128)(2,1)S(1)}, bf16[128,256]{1,0:T(8,128)(2,1)S(1)}, u32[]{:S(2)}, u32[]{:S(2)}) collective-permute-start(bf16[128,256]{1,0:T(8,128)(2,1)S(1)} %get-tuple-element.67), channel_id=1, source_target_pairs={{0,12},{1,13},{2,14},{3,15},{4,8},{5,9},{6,10},{7,11},{8,4},{9,5},... | collective-permute-start | bytes 196616 | tf_op jit(solution)/shard_map/ppermute | solution.py:420
  63.1 13.7 %collective-permute-start.29 = (bf16[128,256]{1,0:T(8,128)(2,1)S(1)}, bf16[128,256]{1,0:T(8,128)(2,1)S(1)}, u32[]{:S(2)}, u32[]{:S(2)}) collective-permute-start(bf16[128,256]{1,0:T(8,128)(2,1)S(1)} %get-tuple-element.68), channel_id=1, source_target_pairs={{0,13},{1,12},{2,15},{3,14},{4,9},{5,8},{6,11},{7,10},{8,5},{9,4},... | collective-permute-start | bytes 196616 | tf_op jit(solution)/shard_map/ppermute | solution.py:420
  69.9 8.2 %collective-permute-start.30 = (bf16[128,256]{1,0:T(8,128)(2,1)S(1)}, bf16[128,256]{1,0:T(8,128)(2,1)S(1)}, u32[]{:S(2)}, u32[]{:S(2)}) collective-permute-start(bf16[128,256]{1,0:T(8,128)(2,1)S(1)} %get-tuple-element.69), channel_id=1, source_target_pairs={{0,14},{1,15},{2,12},{3,13},{4,10},{5,11},{6,8},{7,9},{8,6},{9,7},... | collective-permute-start | bytes 196616 | tf_op jit(solution)/shard_map/ppermute | solution.py:420
  71.7 10.2 %collective-permute-start.31 = (bf16[128,256]{1,0:T(8,128)(2,1)S(1)}, bf16[128,256]{1,0:T(8,128)(2,1)S(1)}, u32[]{:S(2)}, u32[]{:S(2)}) collective-permute-start(bf16[128,256]{1,0:T(8,128)(2,1)S(1)} %get-tuple-element.70), channel_id=1, source_target_pairs={{0,15},{1,14},{2,13},{3,12},{4,11},{5,10},{6,9},{7,8},{8,7},{9,6},... | collective-permute-start | bytes 196616 | tf_op jit(solution)/shard_map/ppermute | solution.py:420
  74.1 11.5 %collective-permute-start.5 = (bf16[120,256]{1,0:T(8,128)(2,1)S(1)}, bf16[120,256]{1,0:T(8,128)(2,1)S(1)}, u32[]{:S(2)}, u32[]{:S(2)}) collective-permute-start(bf16[120,256]{1,0:T(8,128)(2,1)S(1)} %get-tuple-element.44), channel_id=1, source_target_pairs={{0,4},{1,5},{2,6},{3,7},{4,0},{5,1},{6,2},{7,3},{8,12},{9,13},{10,... | collective-permute-start | bytes 184328 | tf_op jit(solution)/shard_map/ppermute | solution.py:420
  74.1 11.5 %collective-permute-start.6 = (bf16[120,256]{1,0:T(8,128)(2,1)S(1)}, bf16[120,256]{1,0:T(8,128)(2,1)S(1)}, u32[]{:S(2)}, u32[]{:S(2)}) collective-permute-start(bf16[120,256]{1,0:T(8,128)(2,1)S(1)} %get-tuple-element.45), channel_id=1, source_target_pairs={{0,5},{1,4},{2,7},{3,6},{4,1},{5,0},{6,3},{7,2},{8,13},{9,12},{10,... | collective-permute-start | bytes 184328 | tf_op jit(solution)/shard_map/ppermute | solution.py:420
  76.8 8.9 %collective-permute-start.7 = (bf16[120,256]{1,0:T(8,128)(2,1)S(1)}, bf16[120,256]{1,0:T(8,128)(2,1)S(1)}, u32[]{:S(2)}, u32[]{:S(2)}) collective-permute-start(bf16[120,256]{1,0:T(8,128)(2,1)S(1)} %get-tuple-element.46), channel_id=1, source_target_pairs={{0,6},{1,7},{2,4},{3,5},{4,2},{5,3},{6,0},{7,1},{8,14},{9,15},{10,... | collective-permute-start | bytes 184328 | tf_op jit(solution)/shard_map/ppermute | solution.py:420
  78.1 7.6 %collective-permute-start.8 = (bf16[120,256]{1,0:T(8,128)(2,1)S(1)}, bf16[120,256]{1,0:T(8,128)(2,1)S(1)}, u32[]{:S(2)}, u32[]{:S(2)}) collective-permute-start(bf16[120,256]{1,0:T(8,128)(2,1)S(1)} %get-tuple-element.47), channel_id=1, source_target_pairs={{0,7},{1,6},{2,5},{3,4},{4,3},{5,2},{6,1},{7,0},{8,15},{9,14},{10,... | collective-permute-start | bytes 184328 | tf_op jit(solution)/shard_map/ppermute | solution.py:420
  (11 other events, 113.9 us)
